TPU v7x, 256 devices: a whole 4x4x8 slice. The times are simulated.
256 devices in a mesh: gx: 16 (over z, core), gy: 4 (over y), gz: 4 (over x).
Axes of the slice: x: 4, y: 4, z: 8, core: 2. Of those that a mesh axis runs over, the one named last changes fastest.
Arguments:
- start_state: float32 [16, 64, 32, 512], P(None, 'gx', 'gz', 'gy'), may hold values from -6 to 6
- cotangent: float32 [16, 64, 32, 512], P(None, 'gx', 'gz', 'gy'), may hold values from -6 to 6
- update_masks: int32 [2, 64, 32, 512], P(None, 'gx', 'gz', 'gy'), may hold values 0 or 1
- first_weight: float32 [48, 64], replicated, may hold values from -0.875 to 0.875
- first_bias: float32 [64], replicated, may hold values from -3 to 3
- second_weight: float32 [64, 16], replicated, may hold values from -0.75 to 0.75
- second_bias: float32 [16], replicated, may hold values from -3 to 3
Outputs:
- grad_state: float32 [16, 64, 32, 512], P(None, 'gx', 'gz', 'gy')
- grad_first_weight: float32 [48, 64], replicated
- grad_first_bias: float32 [64], replicated
- grad_second_weight: float32 [64, 16], replicated
- grad_second_bias: float32 [16], replicated
Inputs may be any that keep to these rules, and one draw needn't show every extreme that they name: `update_masks`: a flag for each cell and step.
All inputs are finite; a program needn't handle non-finite values. No bound on the sum of `update_masks` on one device may be relied on, other than what follows from the above.
Results may differ from a plain program's by a relative error of at most 0.0003.
Values sent between devices are 32-bit elements; how exact they have to be, the bound alone decides.
A program may use at most 64 MiB of HBM per device.

v0:
```python
import math

import jax
import jax.numpy as jnp
from jax import lax
from jax.sharding import PartitionSpec as P

highest = lax.Precision.HIGHEST


def extended(value, sides, width):
    for axis, dim in sides:
        count, length = (lax.axis_size(axis), value.shape[dim])
        up = [(i, (i + 1) % count) for i in range(count - 1)]
        down = [(j, i) for i, j in up]
        last = lax.slice_in_dim(value, length - width, length, axis=dim)
        initial = lax.slice_in_dim(value, 0, width, axis=dim)
        before = lax.ppermute(last, axis, up)
        after = lax.ppermute(initial, axis, down)
        value = jnp.concatenate([before, value, after], axis=dim)
    return value


def shifted(field, axis, start):
    return lax.slice_in_dim(field, start, field.shape[axis] - 2 + start, axis=axis)


def differ(field, axis):
    return shifted(field, axis, 2) - shifted(field, axis, 0)


def smooth(field, axis):
    return shifted(field, axis, 0) + 2.0 * shifted(field, axis, 1) + shifted(field, axis, 2)


def along_x(field):
    return smooth(smooth(differ(field, 1), 2), 3) * 0.125


def along_y(field):
    return smooth(smooth(differ(field, 3), 1), 2) * 0.125


def along_z(field):
    return smooth(smooth(differ(field, 2), 1), 3) * 0.125


def sobel(field):
    return jnp.concatenate([along_x(field), along_y(field), along_z(field)], axis=0)


def sobel_adjoint(grads, chans):
    return -(
        along_x(grads[:chans]) + along_y(grads[chans : 2 * chans]) + along_z(grads[2 * chans :])
    )


def hidden_of(perc, first_weight, first_bias):
    return jnp.tanh(
        jnp.einsum("kh,kxzy->hxzy", first_weight, perc, precision=highest)
        + first_bias[:, None, None, None]
    )


def update_of(hidden, second_weight, second_bias):
    return (
        jnp.einsum("ho,hxzy->oxzy", second_weight, hidden, precision=highest)
        + second_bias[:, None, None, None]
    )


def backward_cells(perc, hidden, masked, first_weight, second_weight):
    hid_grad = jnp.einsum("ho,oxzy->hxzy", second_weight, masked, precision=highest)
    pre_grad = hid_grad * (1.0 - hidden * hidden)
    perc_grad = jnp.einsum("kh,hxzy->kxzy", first_weight, pre_grad, precision=highest)
    grads = (
        jnp.einsum("kxzy,hxzy->kh", perc, pre_grad, precision=highest),
        jnp.sum(pre_grad, axis=(1, 2, 3)),
        jnp.einsum("hxzy,oxzy->ho", hidden, masked, precision=highest),
        jnp.sum(masked, axis=(1, 2, 3)),
    )
    return (perc_grad, grads)


def body(
    start_state, cotangent, update_masks, first_weight, first_bias, second_weight, second_bias
):
    chans = start_state.shape[0]
    steps_count = update_masks.shape[0]
    total_cells = (
        start_state.shape[1]
        * start_state.shape[2]
        * start_state.shape[3]
        * lax.axis_size("gx")
        * lax.axis_size("gy")
        * lax.axis_size("gz")
    )
    scale = 1.0 / math.sqrt(total_cells)
    masks_float = update_masks.astype(jnp.float32)
    totals = None
    carried = cotangent
    current = start_state
    saved = []
    for step in range(steps_count):
        padded = extended(current, (("gx", 1), ("gy", 3), ("gz", 2)), 1)
        perc = sobel(padded)
        hidden = hidden_of(perc, first_weight, first_bias)
        saved.append((perc, hidden))
        if step + 1 < steps_count:
            current = current + masks_float[step][None] * update_of(
                hidden, second_weight, second_bias
            )
    for step in range(steps_count - 1, -1, -1):
        perc, hidden = saved[step]
        masked = masks_float[step][None] * carried
        perc_grad, grads = backward_cells(perc, hidden, masked, first_weight, second_weight)
        totals = grads if totals is None else tuple((a + b for a, b in zip(totals, grads)))
        padded_grad = extended(perc_grad, (("gx", 1), ("gy", 3), ("gz", 2)), 1)
        carried = carried + sobel_adjoint(padded_grad, chans)
    summed = lax.psum((totals[0], totals[1], totals[2], totals[3]), ("gx", "gy", "gz"))
    return (carried, summed[0] * scale, summed[1] * scale, summed[2] * scale, summed[3] * scale)


def solution(mesh):
    in_specs = (
        P(None, "gx", "gz", "gy"),
        P(None, "gx", "gz", "gy"),
        P(None, "gx", "gz", "gy"),
        P(),
        P(),
        P(),
        P(),
    )
    out_specs = (P(None, "gx", "gz", "gy"), P(), P(), P(), P())
    return jax.shard_map(body, mesh=mesh, in_specs=in_specs, out_specs=out_specs, check_vma=False)
```

profile of v0, /device:TPU:1, one launch (start us, length us, event | category | flops | bytes accessed | tf_op | source)
XLA Modules:
  0.0 237.2 jit_solution(2468843388477532681)
XLA Ops:
  1.6 4.9 %collective-permute-start = (f32[16,1,8,128]{3,0,2,1:T(8,128)S(1)}, f32[16,1,8,128]{3,0,2,1:T(8,128)S(1)}, u32[]{:S(2)}, u32[]{:S(2)}) collective-permute-start(f32[16,1,8,128]{3,0,2,1:T(8,128)S(1)} %copy.49), channel_id=1, source_target_pairs={{0,16},{16,32},{32,48},{48,64},{64,80},{80,96},{96,112},{112,128},... | collective-permute-start | bytes 196616 | tf_op jit(solution)/shard_map/ppermute | solution.py:18
  6.5 1.9 collective-permute-start.1
  8.5 1.1 constant_dynamic-update-slice_fusion.1
  9.6 2.5 %collective-permute-done.1 = f32[16,1,8,128]{3,0,2,1:T(8,128)S(1)} collective-permute-done((f32[16,1,8,128]{3,0,2,1:T(8,128)S(1)}, f32[16,1,8,128]{3,0,2,1:T(8,128)S(1)}, u32[]{:S(2)}, u32[]{:S(2)}) %collective-permute-start.1) | collective-permute-done | bytes 65568 | tf_op jit(solution)/shard_map/ppermute | solution.py:19
  12.3 3.2 %collective-permute-start.2 = (f32[16,6,8,1]{3,0,2,1:T(8,128)S(1)}, f32[16,6,8,1]{3,0,2,1:T(8,128)S(1)}, u32[]{:S(2)}, u32[]{:S(2)}) collective-permute-start(f32[16,6,8,1]{3,0,2,1:T(8,128)S(1)} %get-tuple-element.41), channel_id=1, source_target_pairs={{0,4},{4,8},{8,12},{1,5},{5,9},{9,13},{2,6},{6,10},{10,14},{3,7},{... | collective-permute-start | bytes 9224 | tf_op jit(solution)/shard_map/ppermute | solution.py:18
  15.5 1.3 collective-permute-start.3
  16.9 5.6 %collective-permute-done.2 = f32[16,6,8,1]{3,0,2,1:T(8,128)S(1)} collective-permute-done((f32[16,6,8,1]{3,0,2,1:T(8,128)S(1)}, f32[16,6,8,1]{3,0,2,1:T(8,128)S(1)}, u32[]{:S(2)}, u32[]{:S(2)}) %collective-permute-start.2) | collective-permute-done | bytes 3104 | tf_op jit(solution)/shard_map/ppermute | solution.py:18
  22.5 4.1 %collective-permute-done.3 = f32[16,6,8,1]{3,0,2,1:T(8,128)S(1)} collective-permute-done((f32[16,6,8,1]{3,0,2,1:T(8,128)S(1)}, f32[16,6,8,1]{3,0,2,1:T(8,128)S(1)}, u32[]{:S(2)}, u32[]{:S(2)}) %collective-permute-start.3) | collective-permute-done | bytes 3104 | tf_op jit(solution)/shard_map/ppermute | solution.py:19
  26.7 1.3 collective-permute-start.5
  28.0 4.0 %collective-permute-start.4 = (f32[16,6,1,130]{3,0,2,1:T(8,128)S(1)}, f32[16,6,1,130]{3,0,2,1:T(8,128)S(1)}, u32[]{:S(2)}, u32[]{:S(2)}) collective-permute-start(f32[16,6,1,130]{3,0,2,1:T(8,128)S(1)} %get-tuple-element.34), channel_id=1, source_target_pairs={{0,1},{1,2},{2,3},{4,5},{5,6},{6,7},{8,9},{9,10},{10,11},{12,13},{... | collective-permute-start | bytes 149768 | tf_op jit(solution)/shard_map/ppermute | solution.py:18
  32.6 1.8 collective-permute-done.4
  36.7 1.0 fusion.3
  38.6 5.0 %collective-permute-start.6 = (f32[16,1,8,128]{3,0,2,1:T(8,128)S(1)}, f32[16,1,8,128]{3,0,2,1:T(8,128)S(1)}, u32[]{:S(2)}, u32[]{:S(2)}) collective-permute-start(f32[16,1,8,128]{3,0,2,1:T(8,128)S(1)} %get-tuple-element.43), channel_id=1, source_target_pairs={{0,16},{16,32},{32,48},{48,64},{64,80},{80,96},{96,112},{112,128},... | collective-permute-start | bytes 196616 | tf_op jit(solution)/shard_map/ppermute | solution.py:18
  43.6 1.9 collective-permute-start.7
  45.5 3.6 %collective-permute-done.7 = f32[16,1,8,128]{3,0,2,1:T(8,128)S(1)} collective-permute-done((f32[16,1,8,128]{3,0,2,1:T(8,128)S(1)}, f32[16,1,8,128]{3,0,2,1:T(8,128)S(1)}, u32[]{:S(2)}, u32[]{:S(2)}) %collective-permute-start.7) | collective-permute-done | bytes 65568 | tf_op jit(solution)/shard_map/ppermute | solution.py:19
  49.4 3.2 %collective-permute-start.8 = (f32[16,6,8,1]{3,0,2,1:T(8,128)S(1)}, f32[16,6,8,1]{3,0,2,1:T(8,128)S(1)}, u32[]{:S(2)}, u32[]{:S(2)}) collective-permute-start(f32[16,6,8,1]{3,0,2,1:T(8,128)S(1)} %get-tuple-element.39), channel_id=1, source_target_pairs={{0,4},{4,8},{8,12},{1,5},{5,9},{9,13},{2,6},{6,10},{10,14},{3,7},{... | collective-permute-start | bytes 9224 | tf_op jit(solution)/shard_map/ppermute | solution.py:18
  52.6 1.3 collective-permute-start.9
  53.9 5.6 %collective-permute-done.8 = f32[16,6,8,1]{3,0,2,1:T(8,128)S(1)} collective-permute-done((f32[16,6,8,1]{3,0,2,1:T(8,128)S(1)}, f32[16,6,8,1]{3,0,2,1:T(8,128)S(1)}, u32[]{:S(2)}, u32[]{:S(2)}) %collective-permute-start.8) | collective-permute-done | bytes 3104 | tf_op jit(solution)/shard_map/ppermute | solution.py:18
  59.5 4.1 %collective-permute-done.9 = f32[16,6,8,1]{3,0,2,1:T(8,128)S(1)} collective-permute-done((f32[16,6,8,1]{3,0,2,1:T(8,128)S(1)}, f32[16,6,8,1]{3,0,2,1:T(8,128)S(1)}, u32[]{:S(2)}, u32[]{:S(2)}) %collective-permute-start.9) | collective-permute-done | bytes 3104 | tf_op jit(solution)/shard_map/ppermute | solution.py:19
  63.8 1.3 collective-permute-start.11
  65.1 4.7 %collective-permute-start.10 = (f32[16,6,1,130]{3,0,2,1:T(8,128)S(1)}, f32[16,6,1,130]{3,0,2,1:T(8,128)S(1)}, u32[]{:S(2)}, u32[]{:S(2)}) collective-permute-start(f32[16,6,1,130]{3,0,2,1:T(8,128)S(1)} %get-tuple-element.32), channel_id=1, source_target_pairs={{0,1},{1,2},{2,3},{4,5},{5,6},{6,7},{8,9},{9,10},{10,11},{12,13},{... | collective-permute-start | bytes 149768 | tf_op jit(solution)/shard_map/ppermute | solution.py:18
  70.1 1.8 collective-permute-done.10
  74.1 1.0 fusion.1
  75.2 1.3 fusion.84
  77.5 5.3 %collective-permute-start.12 = (f32[48,1,8,128]{3,0,2,1:T(8,128)S(1)}, f32[48,1,8,128]{3,0,2,1:T(8,128)S(1)}, u32[]{:S(2)}, u32[]{:S(2)}) collective-permute-start(f32[48,1,8,128]{3,0,2,1:T(8,128)S(1)} %get-tuple-element.37), channel_id=1, source_target_pairs={{0,16},{16,32},{32,48},{48,64},{64,80},{80,96},{96,112},{112,128},... | collective-permute-start | bytes 589832 | tf_op jit(solution)/shard_map/ppermute | solution.py:18
  82.8 1.9 collective-permute-start.13
  85.4 4.4 %collective-permute-done.13 = f32[48,1,8,128]{3,0,2,1:T(8,128)S(1)} collective-permute-done((f32[48,1,8,128]{3,0,2,1:T(8,128)S(1)}, f32[48,1,8,128]{3,0,2,1:T(8,128)S(1)}, u32[]{:S(2)}, u32[]{:S(2)}) %collective-permute-start.13) | collective-permute-done | bytes 196640 | tf_op jit(solution)/shard_map/ppermute | solution.py:19
  91.4 2.9 %collective-permute-start.14 = (f32[48,6,8,1]{0,2,3,1:T(8,128)S(1)}, f32[48,6,8,1]{0,2,3,1:T(8,128)S(1)}, u32[]{:S(2)}, u32[]{:S(2)}) collective-permute-start(f32[48,6,8,1]{0,2,3,1:T(8,128)S(1)} %copy.25), channel_id=1, source_target_pairs={{0,4},{4,8},{8,12},{1,5},{5,9},{9,13},{2,6},{6,10},{10,14},{3,7},{... | collective-permute-start | bytes 27656 | tf_op jit(solution)/shard_map/ppermute | solution.py:18
  94.7 1.3 collective-permute-start.15
  96.5 2.8 %collective-permute-done.15 = f32[48,6,8,1]{0,2,3,1:T(8,128)S(1)} collective-permute-done((f32[48,6,8,1]{0,2,3,1:T(8,128)S(1)}, f32[48,6,8,1]{0,2,3,1:T(8,128)S(1)}, u32[]{:S(2)}, u32[]{:S(2)}) %collective-permute-start.15) | collective-permute-done | bytes 9248 | tf_op jit(solution)/shard_map/ppermute | solution.py:19
  99.8 1.2 pad_maximum_fusion.64
  100.9 1.4 collective-permute-start.17
  102.4 4.9 %collective-permute-start.16 = (f32[48,6,1,130]{3,0,2,1:T(8,128)S(1)}, f32[48,6,1,130]{3,0,2,1:T(8,128)S(1)}, u32[]{:S(2)}, u32[]{:S(2)}) collective-permute-start(f32[48,6,1,130]{3,0,2,1:T(8,128)S(1)} %get-tuple-element.26), channel_id=1, source_target_pairs={{0,1},{1,2},{2,3},{4,5},{5,6},{6,7},{8,9},{9,10},{10,11},{12,13},{... | collective-permute-start | bytes 449288 | tf_op jit(solution)/shard_map/ppermute | solution.py:18
  108.3 2.1 collective-permute-done.17
  110.4 1.8 collective-permute-done.16
  116.1 1.3 fusion.85
  120.3 1.0 fusion.9
  121.3 79.9 %all-reduce = (f32[48,64]{1,0:T(8,128)S(1)}, f32[64]{0:T(128)S(1)}, f32[64,16]{0,1:T(8,128)S(1)}, f32[16]{0:T(128)S(1)}) all-reduce(f32[48,64]{1,0:T(8,128)S(1)} %fusion.9, f32[64]{0:T(128)S(1)} %add.275, f32[64,16]{0,1:T(8,128)S(1)} %fusion.10, f32[16]{0:T(128)S(1)} %add.277), channel_id=1, replica_groups=mesh['gx'=16,'gy'=4,'gz'=4] {'gx','gy','gz'}, use_global_device_ids=true, to_apply=%region_0.0 | all-reduce | flops 4176 | bytes 33408 | tf_op jit(solution)/shard_map/psum | solution.py:120
  201.9 3.9 %collective-permute-start.18 = (f32[48,1,8,128]{3,0,2,1:T(8,128)S(1)}, f32[48,1,8,128]{3,0,2,1:T(8,128)S(1)}, u32[]{:S(2)}, u32[]{:S(2)}) collective-permute-start(f32[48,1,8,128]{3,0,2,1:T(8,128)S(1)} %get-tuple-element.35), channel_id=1, source_target_pairs={{0,16},{16,32},{32,48},{48,64},{64,80},{80,96},{96,112},{112,128},... | collective-permute-start | bytes 589832 | tf_op jit(solution)/shard_map/ppermute | solution.py:18
  205.8 1.9 collective-permute-start.19
  208.3 4.4 %collective-permute-done.19 = f32[48,1,8,128]{3,0,2,1:T(8,128)S(1)} collective-permute-done((f32[48,1,8,128]{3,0,2,1:T(8,128)S(1)}, f32[48,1,8,128]{3,0,2,1:T(8,128)S(1)}, u32[]{:S(2)}, u32[]{:S(2)}) %collective-permute-start.19) | collective-permute-done | bytes 196640 | tf_op jit(solution)/shard_map/ppermute | solution.py:19
  214.8 1.3 collective-permute-start.21
  216.1 4.0 %collective-permute-start.20 = (f32[48,6,8,1]{0,2,3,1:T(8,128)S(1)}, f32[48,6,8,1]{0,2,3,1:T(8,128)S(1)}, u32[]{:S(2)}, u32[]{:S(2)}) collective-permute-start(f32[48,6,8,1]{0,2,3,1:T(8,128)S(1)} %copy.30), channel_id=1, source_target_pairs={{0,4},{4,8},{8,12},{1,5},{5,9},{9,13},{2,6},{6,10},{10,14},{3,7},{... | collective-permute-start | bytes 27656 | tf_op jit(solution)/shard_map/ppermute | solution.py:18
  221.9 1.1 pad_maximum_fusion.59
  223.1 1.3 collective-permute-start.23
  224.4 4.0 %collective-permute-start.22 = (f32[48,6,1,130]{3,0,2,1:T(8,128)S(1)}, f32[48,6,1,130]{3,0,2,1:T(8,128)S(1)}, u32[]{:S(2)}, u32[]{:S(2)}) collective-permute-start(f32[48,6,1,130]{3,0,2,1:T(8,128)S(1)} %get-tuple-element.24), channel_id=1, source_target_pairs={{0,1},{1,2},{2,3},{4,5},{5,6},{6,7},{8,9},{9,10},{10,11},{12,13},{... | collective-permute-start | bytes 449288 | tf_op jit(solution)/shard_map/ppermute | solution.py:18
  228.9 2.8 %collective-permute-done.23 = f32[48,6,1,130]{3,0,2,1:T(8,128)S(1)} collective-permute-done((f32[48,6,1,130]{3,0,2,1:T(8,128)S(1)}, f32[48,6,1,130]{3,0,2,1:T(8,128)S(1)}, u32[]{:S(2)}, u32[]{:S(2)}) %collective-permute-start.23) | collective-permute-done | bytes 149792 | tf_op jit(solution)/shard_map/ppermute | solution.py:19
  231.6 1.8 collective-permute-done.22
  (151 shorter events, 29.2 us)
Async XLA Ops:
  0.6 35.6 %copy-start = (f32[48,64]{1,0:T(8,128)S(1)}, f32[48,64]{1,0:T(8,128)}, u32[]{:S(2)}) copy-start(f32[48,64]{1,0:T(8,128)} %param.10) | copy-start | bytes 36868
  1.6 6.9 %collective-permute-start = (f32[16,1,8,128]{3,0,2,1:T(8,128)S(1)}, f32[16,1,8,128]{3,0,2,1:T(8,128)S(1)}, u32[]{:S(2)}, u32[]{:S(2)}) collective-permute-start(f32[16,1,8,128]{3,0,2,1:T(8,128)S(1)} %copy.49), channel_id=1, source_target_pairs={{0,16},{16,32},{32,48},{48,64},{64,80},{80,96},{96,112},{112,128},... | collective-permute-start | bytes 196616 | tf_op jit(solution)/shard_map/ppermute | solution.py:18
  6.5 10.3 %copy-start.31 = (s32[2,4,8,128]{3,2,1,0:T(8,128)S(1)}, s32[2,4,8,128]{3,2,1,0:T(8,128)}, u32[]{:S(2)}) copy-start(s32[2,4,8,128]{3,2,1,0:T(8,128)} %param.9) | copy-start | bytes 98308
  6.5 5.6 %collective-permute-start.1 = (f32[16,1,8,128]{3,0,2,1:T(8,128)S(1)}, f32[16,1,8,128]{3,0,2,1:T(8,128)S(1)}, u32[]{:S(2)}, u32[]{:S(2)}) collective-permute-start(f32[16,1,8,128]{3,0,2,1:T(8,128)S(1)} %copy.50), channel_id=1, source_target_pairs={{16,0},{32,16},{48,32},{64,48},{80,64},{96,80},{112,96},{128,112},... | collective-permute-start | bytes 196616 | tf_op jit(solution)/shard_map/ppermute | solution.py:19
  12.3 10.2 %collective-permute-start.2 = (f32[16,6,8,1]{3,0,2,1:T(8,128)S(1)}, f32[16,6,8,1]{3,0,2,1:T(8,128)S(1)}, u32[]{:S(2)}, u32[]{:S(2)}) collective-permute-start(f32[16,6,8,1]{3,0,2,1:T(8,128)S(1)} %get-tuple-element.41), channel_id=1, source_target_pairs={{0,4},{4,8},{8,12},{1,5},{5,9},{9,13},{2,6},{6,10},{10,14},{3,7},{... | collective-permute-start | bytes 9224 | tf_op jit(solution)/shard_map/ppermute | solution.py:18
  15.5 11.1 %collective-permute-start.3 = (f32[16,6,8,1]{3,0,2,1:T(8,128)S(1)}, f32[16,6,8,1]{3,0,2,1:T(8,128)S(1)}, u32[]{:S(2)}, u32[]{:S(2)}) collective-permute-start(f32[16,6,8,1]{3,0,2,1:T(8,128)S(1)} %get-tuple-element.42), channel_id=1, source_target_pairs={{4,0},{8,4},{12,8},{5,1},{9,5},{13,9},{6,2},{10,6},{14,10},{7,3},{... | collective-permute-start | bytes 9224 | tf_op jit(solution)/shard_map/ppermute | solution.py:19
  26.7 5.8 %collective-permute-start.5 = (f32[16,6,1,130]{3,0,2,1:T(8,128)S(1)}, f32[16,6,1,130]{3,0,2,1:T(8,128)S(1)}, u32[]{:S(2)}, u32[]{:S(2)}) collective-permute-start(f32[16,6,1,130]{3,0,2,1:T(8,128)S(1)} %get-tuple-element.33), channel_id=1, source_target_pairs={{1,0},{2,1},{3,2},{5,4},{6,5},{7,6},{9,8},{10,9},{11,10},{13,12},{... | collective-permute-start | bytes 149768 | tf_op jit(solution)/shard_map/ppermute | solution.py:19
  28.0 6.3 %collective-permute-start.4 = (f32[16,6,1,130]{3,0,2,1:T(8,128)S(1)}, f32[16,6,1,130]{3,0,2,1:T(8,128)S(1)}, u32[]{:S(2)}, u32[]{:S(2)}) collective-permute-start(f32[16,6,1,130]{3,0,2,1:T(8,128)S(1)} %get-tuple-element.34), channel_id=1, source_target_pairs={{0,1},{1,2},{2,3},{4,5},{5,6},{6,7},{8,9},{9,10},{10,11},{12,13},{... | collective-permute-start | bytes 149768 | tf_op jit(solution)/shard_map/ppermute | solution.py:18
  36.0 1.7 copy-start.13
  36.2 2.3 copy-start.23
  36.2 2.3 copy-start.25
  36.2 1.5 copy-start.27
  36.2 1.5 copy-start.30
  36.3 1.5 copy-start.33
  37.7 11.5 %copy-start.1 = (f32[64,4,8,128]{3,0,2,1:T(8,128)}, f32[64,4,8,128]{3,0,2,1:T(8,128)S(1)}, u32[]{:S(2)}) copy-start(f32[64,4,8,128]{3,0,2,1:T(8,128)S(1)} %fusion.3) | copy-start | bytes 3145732
  38.6 6.9 %collective-permute-start.6 = (f32[16,1,8,128]{3,0,2,1:T(8,128)S(1)}, f32[16,1,8,128]{3,0,2,1:T(8,128)S(1)}, u32[]{:S(2)}, u32[]{:S(2)}) collective-permute-start(f32[16,1,8,128]{3,0,2,1:T(8,128)S(1)} %get-tuple-element.43), channel_id=1, source_target_pairs={{0,16},{16,32},{32,48},{48,64},{64,80},{80,96},{96,112},{112,128},... | collective-permute-start | bytes 196616 | tf_op jit(solution)/shard_map/ppermute | solution.py:18
  43.6 5.6 %collective-permute-start.7 = (f32[16,1,8,128]{3,0,2,1:T(8,128)S(1)}, f32[16,1,8,128]{3,0,2,1:T(8,128)S(1)}, u32[]{:S(2)}, u32[]{:S(2)}) collective-permute-start(f32[16,1,8,128]{3,0,2,1:T(8,128)S(1)} %get-tuple-element.44), channel_id=1, source_target_pairs={{16,0},{32,16},{48,32},{64,48},{80,64},{96,80},{112,96},{128,112},... | collective-permute-start | bytes 196616 | tf_op jit(solution)/shard_map/ppermute | solution.py:19
  49.2 20.7 %copy-start.28 = (f32[16,4,8,128]{3,2,1,0:T(8,128)S(1)}, f32[16,4,8,128]{3,2,1,0:T(8,128)}, u32[]{:S(2)}) copy-start(f32[16,4,8,128]{3,2,1,0:T(8,128)} %param.8) | copy-start | bytes 786436
  49.4 10.1 %collective-permute-start.8 = (f32[16,6,8,1]{3,0,2,1:T(8,128)S(1)}, f32[16,6,8,1]{3,0,2,1:T(8,128)S(1)}, u32[]{:S(2)}, u32[]{:S(2)}) collective-permute-start(f32[16,6,8,1]{3,0,2,1:T(8,128)S(1)} %get-tuple-element.39), channel_id=1, source_target_pairs={{0,4},{4,8},{8,12},{1,5},{5,9},{9,13},{2,6},{6,10},{10,14},{3,7},{... | collective-permute-start | bytes 9224 | tf_op jit(solution)/shard_map/ppermute | solution.py:18
  52.6 11.1 %collective-permute-start.9 = (f32[16,6,8,1]{3,0,2,1:T(8,128)S(1)}, f32[16,6,8,1]{3,0,2,1:T(8,128)S(1)}, u32[]{:S(2)}, u32[]{:S(2)}) collective-permute-start(f32[16,6,8,1]{3,0,2,1:T(8,128)S(1)} %get-tuple-element.40), channel_id=1, source_target_pairs={{4,0},{8,4},{12,8},{5,1},{9,5},{13,9},{6,2},{10,6},{14,10},{7,3},{... | collective-permute-start | bytes 9224 | tf_op jit(solution)/shard_map/ppermute | solution.py:19
  63.8 6.3 %collective-permute-start.11 = (f32[16,6,1,130]{3,0,2,1:T(8,128)S(1)}, f32[16,6,1,130]{3,0,2,1:T(8,128)S(1)}, u32[]{:S(2)}, u32[]{:S(2)}) collective-permute-start(f32[16,6,1,130]{3,0,2,1:T(8,128)S(1)} %get-tuple-element.31), channel_id=1, source_target_pairs={{1,0},{2,1},{3,2},{5,4},{6,5},{7,6},{9,8},{10,9},{11,10},{13,12},{... | collective-permute-start | bytes 149768 | tf_op jit(solution)/shard_map/ppermute | solution.py:19
  65.1 6.7 %collective-permute-start.10 = (f32[16,6,1,130]{3,0,2,1:T(8,128)S(1)}, f32[16,6,1,130]{3,0,2,1:T(8,128)S(1)}, u32[]{:S(2)}, u32[]{:S(2)}) collective-permute-start(f32[16,6,1,130]{3,0,2,1:T(8,128)S(1)} %get-tuple-element.32), channel_id=1, source_target_pairs={{0,1},{1,2},{2,3},{4,5},{5,6},{6,7},{8,9},{9,10},{10,11},{12,13},{... | collective-permute-start | bytes 149768 | tf_op jit(solution)/shard_map/ppermute | solution.py:18
  70.1 5.1 %copy-start.21 = (f32[16,4,8,128]{3,2,1,0:T(8,128)}, f32[16,4,8,128]{3,2,1,0:T(8,128)S(1)}, u32[]{:S(2)}) copy-start(f32[16,4,8,128]{3,2,1,0:T(8,128)S(1)} %get-tuple-element.22) | copy-start | bytes 786436
  73.7 1.4 copy-start.17
  75.2 1.3 copy-start.5
  77.5 7.9 %collective-permute-start.12 = (f32[48,1,8,128]{3,0,2,1:T(8,128)S(1)}, f32[48,1,8,128]{3,0,2,1:T(8,128)S(1)}, u32[]{:S(2)}, u32[]{:S(2)}) collective-permute-start(f32[48,1,8,128]{3,0,2,1:T(8,128)S(1)} %get-tuple-element.37), channel_id=1, source_target_pairs={{0,16},{16,32},{32,48},{48,64},{64,80},{80,96},{96,112},{112,128},... | collective-permute-start | bytes 589832 | tf_op jit(solution)/shard_map/ppermute | solution.py:18
  82.8 7.0 %collective-permute-start.13 = (f32[48,1,8,128]{3,0,2,1:T(8,128)S(1)}, f32[48,1,8,128]{3,0,2,1:T(8,128)S(1)}, u32[]{:S(2)}, u32[]{:S(2)}) collective-permute-start(f32[48,1,8,128]{3,0,2,1:T(8,128)S(1)} %get-tuple-element.38), channel_id=1, source_target_pairs={{16,0},{32,16},{48,32},{64,48},{80,64},{96,80},{112,96},{128,112},... | collective-permute-start | bytes 589832 | tf_op jit(solution)/shard_map/ppermute | solution.py:19
  91.4 4.6 %collective-permute-start.14 = (f32[48,6,8,1]{0,2,3,1:T(8,128)S(1)}, f32[48,6,8,1]{0,2,3,1:T(8,128)S(1)}, u32[]{:S(2)}, u32[]{:S(2)}) collective-permute-start(f32[48,6,8,1]{0,2,3,1:T(8,128)S(1)} %copy.25), channel_id=1, source_target_pairs={{0,4},{4,8},{8,12},{1,5},{5,9},{9,13},{2,6},{6,10},{10,14},{3,7},{... | collective-permute-start | bytes 27656 | tf_op jit(solution)/shard_map/ppermute | solution.py:18
  94.7 4.6 %collective-permute-start.15 = (f32[48,6,8,1]{0,2,3,1:T(8,128)S(1)}, f32[48,6,8,1]{0,2,3,1:T(8,128)S(1)}, u32[]{:S(2)}, u32[]{:S(2)}) collective-permute-start(f32[48,6,8,1]{0,2,3,1:T(8,128)S(1)} %copy.26), channel_id=1, source_target_pairs={{4,0},{8,4},{12,8},{5,1},{9,5},{13,9},{6,2},{10,6},{14,10},{7,3},{... | collective-permute-start | bytes 27656 | tf_op jit(solution)/shard_map/ppermute | solution.py:19
  99.7 7.6 %copy-start.6 = (f32[64,4,8,128]{3,0,2,1:T(8,128)S(1)}, f32[64,4,8,128]{3,0,2,1:T(8,128)}, u32[]{:S(2)}) copy-start(f32[64,4,8,128]{3,0,2,1:T(8,128)} %copy-done.5) | copy-start | bytes 3145732
  99.7 7.6 %copy-start.22 = (f32[16,4,8,128]{3,2,1,0:T(8,128)S(1)}, f32[16,4,8,128]{3,2,1,0:T(8,128)}, u32[]{:S(2)}) copy-start(f32[16,4,8,128]{3,2,1,0:T(8,128)} %copy-done.21) | copy-start | bytes 786436
  100.9 11.2 %copy-start.10 = (f32[48,1,8,128]{3,0,2,1:T(8,128)S(1)}, f32[48,1,8,128]{3,0,2,1:T(8,128)}, u32[]{:S(2)}) copy-start(f32[48,1,8,128]{3,0,2,1:T(8,128)} %copy-done.9) | copy-start | bytes 589828
  100.9 9.5 %collective-permute-start.17 = (f32[48,6,1,130]{3,0,2,1:T(8,128)S(1)}, f32[48,6,1,130]{3,0,2,1:T(8,128)S(1)}, u32[]{:S(2)}, u32[]{:S(2)}) collective-permute-start(f32[48,6,1,130]{3,0,2,1:T(8,128)S(1)} %get-tuple-element.25), channel_id=1, source_target_pairs={{1,0},{2,1},{3,2},{5,4},{6,5},{7,6},{9,8},{10,9},{11,10},{13,12},{... | collective-permute-start | bytes 449288 | tf_op jit(solution)/shard_map/ppermute | solution.py:19
  102.4 9.8 %collective-permute-start.16 = (f32[48,6,1,130]{3,0,2,1:T(8,128)S(1)}, f32[48,6,1,130]{3,0,2,1:T(8,128)S(1)}, u32[]{:S(2)}, u32[]{:S(2)}) collective-permute-start(f32[48,6,1,130]{3,0,2,1:T(8,128)S(1)} %get-tuple-element.26), channel_id=1, source_target_pairs={{0,1},{1,2},{2,3},{4,5},{5,6},{6,7},{8,9},{9,10},{10,11},{12,13},{... | collective-permute-start | bytes 449288 | tf_op jit(solution)/shard_map/ppermute | solution.py:18
  115.3 4.0 %copy-start.11 = (f32[16,4,8,128]{3,0,2,1:T(8,128)}, f32[16,4,8,128]{3,0,2,1:T(8,128)S(1)}, u32[]{:S(2)}) copy-start(f32[16,4,8,128]{3,0,2,1:T(8,128)S(1)} %get-tuple-element.20) | copy-start | bytes 786436
  116.1 1.3 copy-start.24
  116.1 1.3 copy-start.26
  118.3 1.9 copy-start.4
  118.4 1.9 copy-start.16
  118.4 1.9 copy-start.18
  118.4 1.9 copy-start.20
  201.9 6.5 %collective-permute-start.18 = (f32[48,1,8,128]{3,0,2,1:T(8,128)S(1)}, f32[48,1,8,128]{3,0,2,1:T(8,128)S(1)}, u32[]{:S(2)}, u32[]{:S(2)}) collective-permute-start(f32[48,1,8,128]{3,0,2,1:T(8,128)S(1)} %get-tuple-element.35), channel_id=1, source_target_pairs={{0,16},{16,32},{32,48},{48,64},{64,80},{80,96},{96,112},{112,128},... | collective-permute-start | bytes 589832 | tf_op jit(solution)/shard_map/ppermute | solution.py:18
  205.8 7.0 %collective-permute-start.19 = (f32[48,1,8,128]{3,0,2,1:T(8,128)S(1)}, f32[48,1,8,128]{3,0,2,1:T(8,128)S(1)}, u32[]{:S(2)}, u32[]{:S(2)}) collective-permute-start(f32[48,1,8,128]{3,0,2,1:T(8,128)S(1)} %get-tuple-element.36), channel_id=1, source_target_pairs={{16,0},{32,16},{48,32},{64,48},{80,64},{96,80},{112,96},{128,112},... | collective-permute-start | bytes 589832 | tf_op jit(solution)/shard_map/ppermute | solution.py:19
  214.8 6.7 %collective-permute-start.21 = (f32[48,6,8,1]{0,2,3,1:T(8,128)S(1)}, f32[48,6,8,1]{0,2,3,1:T(8,128)S(1)}, u32[]{:S(2)}, u32[]{:S(2)}) collective-permute-start(f32[48,6,8,1]{0,2,3,1:T(8,128)S(1)} %copy.31), channel_id=1, source_target_pairs={{4,0},{8,4},{12,8},{5,1},{9,5},{13,9},{6,2},{10,6},{14,10},{7,3},{... | collective-permute-start | bytes 27656 | tf_op jit(solution)/shard_map/ppermute | solution.py:19
  216.1 4.9 %collective-permute-start.20 = (f32[48,6,8,1]{0,2,3,1:T(8,128)S(1)}, f32[48,6,8,1]{0,2,3,1:T(8,128)S(1)}, u32[]{:S(2)}, u32[]{:S(2)}) collective-permute-start(f32[48,6,8,1]{0,2,3,1:T(8,128)S(1)} %copy.30), channel_id=1, source_target_pairs={{0,4},{4,8},{8,12},{1,5},{5,9},{9,13},{2,6},{6,10},{10,14},{3,7},{... | collective-permute-start | bytes 27656 | tf_op jit(solution)/shard_map/ppermute | solution.py:18
  221.9 11.5 %copy-start.8 = (f32[48,1,8,128]{3,0,2,1:T(8,128)S(1)}, f32[48,1,8,128]{3,0,2,1:T(8,128)}, u32[]{:S(2)}) copy-start(f32[48,1,8,128]{3,0,2,1:T(8,128)} %copy-done.7) | copy-start | bytes 589828
  223.1 8.6 %collective-permute-start.23 = (f32[48,6,1,130]{3,0,2,1:T(8,128)S(1)}, f32[48,6,1,130]{3,0,2,1:T(8,128)S(1)}, u32[]{:S(2)}, u32[]{:S(2)}) collective-permute-start(f32[48,6,1,130]{3,0,2,1:T(8,128)S(1)} %get-tuple-element.23), channel_id=1, source_target_pairs={{1,0},{2,1},{3,2},{5,4},{6,5},{7,6},{9,8},{10,9},{11,10},{13,12},{... | collective-permute-start | bytes 449288 | tf_op jit(solution)/shard_map/ppermute | solution.py:19
  224.4 9.0 %collective-permute-start.22 = (f32[48,6,1,130]{3,0,2,1:T(8,128)S(1)}, f32[48,6,1,130]{3,0,2,1:T(8,128)S(1)}, u32[]{:S(2)}, u32[]{:S(2)}) collective-permute-start(f32[48,6,1,130]{3,0,2,1:T(8,128)S(1)} %get-tuple-element.24), channel_id=1, source_target_pairs={{0,1},{1,2},{2,3},{4,5},{5,6},{6,7},{8,9},{9,10},{10,11},{12,13},{... | collective-permute-start | bytes 449288 | tf_op jit(solution)/shard_map/ppermute | solution.py:18
  (10 other events, 9.2 us)
where the time goes:
time: 240 us; the launch traced here: 237 us
  blocking collectives  79.9 us (33%)
  starting transfers between devices  68.3 us (28%)
  waiting for transfers between devices  50.8 us (21%)
  other arithmetic  13.3 us (6%)
  local copies, waits for them, and re-layouts  12.3 us (5%)
  matrix products  11 us (5%)
    psum x1, blocking collectives, body(): lax.psum((totals[0], totals[1], totals[2], totals[3]), ('gx', 'gy', 'gz'))  79.9 us
    ppermute x12, starting transfers between devices, extended(): before = lax.ppermute(last, axis, up)  50.1 us
    ppermute x12, waiting for transfers between devices, extended(): after = lax.ppermute(initial, axis, down)  31.4 us
    ppermute x12, waiting for transfers between devices, extended(): before = lax.ppermute(last, axis, up)  19.4 us
    ppermute x12, starting transfers between devices, extended(): after = lax.ppermute(initial, axis, down)  18.2 us
    unnamed x73, local copies, waits for them, and re-layouts  6.65 us
    sub x12, other arithmetic, differ(): return shifted(field, axis, 2) - shifted(field, axis, 0)  4.9 us
  transfers between devices with their start and end apart: 24, of which 19 were waited for; matrix products, arithmetic and copies ran while one was open for 2% of the time, Pallas kernels for 0%

commit v1 on v0

v1 whole, which is shorter than its diff:
```python
import functools
import math

import jax
import jax.numpy as jnp
from jax import lax
from jax.experimental import pallas as pl
from jax.experimental.pallas import tpu as pltpu
from jax.sharding import PartitionSpec as P

MESH = pl.DeviceIdType.MESH
F32 = jnp.float32
BF16 = jnp.bfloat16

CH, HID, PERC = 16, 64, 48
BX, BZ, BY = 4, 8, 128
ROW = BZ * BY

P_ROWS = 2 * PERC + 16 + PERC
H_ROWS = 2 * HID + 16 + HID

DIRS = [(dx, dy, dz) for dx in (-1, 0, 1) for dy in (-1, 0, 1) for dz in (-1, 0, 1) if (dx, dy, dz) != (0, 0, 0)]
FLAT = [d for d in DIRS if d[1] == 0]
TALL = [d for d in DIRS if d[1] != 0]


def high(value):
    return value.astype(BF16).astype(F32)


def split3(value):
    first = high(value)
    second = high(value - first)
    return first, second, value - first - second


def span(step, length, kind):
    if step == 0:
        return pl.ds(1, length)
    if kind == "own":
        return pl.ds(1 if step < 0 else length, 1)
    return pl.ds(0 if step < 0 else length + 1, 1)


def dot(a, b):
    return lax.dot_general(a, b, (((1,), (0,)), ((), ())), preferred_element_type=F32)


def dot_nt(a, b):
    return lax.dot_general(a, b, (((1,), (1,)), ((), ())), preferred_element_type=F32)


def kernel(
    sizes,
    state_ref, cot_ref, mask_ref, w1_ref, b1_ref, w2_ref, b2_ref,
    grad_ref, gw1_ref, gb1_ref, gw2_ref, gb2_ref,
    field, packs, halos, outs, opacks, rx, rz, rc, rpacks,
    percs, hids, hidden, dzs, dus, carried, zf, placed, onehot,
    tall, l1, l2, l3, l4, turn, sums, src1, rx1, rx2, rx3,
    send_sem, recv_sem, ar_send, ar_recv,
):
    nx, ny, nz = sizes
    gx, gy, gz = lax.axis_index("gx"), lax.axis_index("gy"), lax.axis_index("gz")

    def device(offset):
        ox, oy, oz = offset
        return (
            lax.rem(gx + (ox % nx), nx) if ox % nx else gx,
            lax.rem(gy + (oy % ny), ny) if oy % ny else gy,
            lax.rem(gz + (oz % nz), nz) if oz % nz else gz,
        )

    plane = [(0, a, b) for a in range(ny) for b in range(nz) if (a, b) != (0, 0)]
    line = [(a, 0, 0) for a in range(1, nx)]
    partners = []
    for o in DIRS + plane + line:
        o = (o[0] % nx, o[1] % ny, o[2] % nz)
        if o not in partners:
            partners.append(o)

    barrier = pltpu.get_barrier_semaphore()
    for o in partners:
        pl.semaphore_signal(barrier, inc=1, device_id=device(o), device_id_type=MESH)

    lane = lax.broadcasted_iota(jnp.int32, (8, 128), 1)
    sub = lax.broadcasted_iota(jnp.int32, (8, 128), 0)
    lane3 = lax.broadcasted_iota(jnp.int32, (1, 1, 128), 2)
    not_first = (lane3 > 0).astype(F32)
    not_last = (lane3 < 127).astype(F32)

    def pack_state(k):
        def body(x, _):
            tile = field[k, x + 1, pl.ds(1, BZ)].reshape(128, 128)
            turned = tile.T
            packs[k, pl.ds(x, 1), :] = turned[0:1, :]
            packs[k, pl.ds(x + 4, 1), :] = turned[127:128, :]
            return 0
        lax.fori_loop(0, BX, body, 0)

    for x in range(BX):
        for z in range(BZ):
            field[0, x + 1, z + 1] = state_ref[pl.ds(x * BZ + z, CH, stride=BX * BZ), :]
    pack_state(0)

    def state_copies(k):
        copies = []
        for d in FLAT:
            i = DIRS.index(d)
            copies.append(pltpu.make_async_remote_copy(
                src_ref=field.at[k, span(d[0], BX, "own"), span(d[2], BZ, "own")],
                dst_ref=field.at[k, span(-d[0], BX, "halo"), span(-d[2], BZ, "halo")],
                send_sem=send_sem.at[k, i], recv_sem=recv_sem.at[k, i],
                device_id=device(d), device_id_type=MESH))
        for d in TALL:
            i = DIRS.index(d)
            copies.append(pltpu.make_async_remote_copy(
                src_ref=packs.at[k],
                dst_ref=halos.at[k, 0 if d[1] > 0 else 1, 1 - d[0], 1 - d[2]],
                send_sem=send_sem.at[k, i], recv_sem=recv_sem.at[k, i],
                device_id=device(d), device_id_type=MESH))
        return copies

    def out_copies(k):
        copies = []
        for d in FLAT:
            i = DIRS.index(d)
            if d[0] and d[2]:
                dst = rc.at[k, pl.ds(0 if d[0] > 0 else 1, 1), pl.ds(0 if d[2] > 0 else 1, 1)]
            elif d[0]:
                dst = rx.at[k, pl.ds(0 if d[0] > 0 else 1, 1)]
            else:
                dst = rz.at[k, :, pl.ds(0 if d[2] > 0 else 1, 1)]
            copies.append(pltpu.make_async_remote_copy(
                src_ref=outs.at[k, span(d[0], BX, "halo"), span(d[2], BZ, "halo")],
                dst_ref=dst,
                send_sem=send_sem.at[2 + k, i], recv_sem=recv_sem.at[2 + k, i],
                device_id=device(d), device_id_type=MESH))
        for d in TALL:
            i = DIRS.index(d)
            copies.append(pltpu.make_async_remote_copy(
                src_ref=opacks.at[k, 0 if d[1] < 0 else 1],
                dst_ref=rpacks.at[k, 0 if d[1] > 0 else 1, 1 - d[0], 1 - d[2]],
                send_sem=send_sem.at[2 + k, i], recv_sem=recv_sem.at[2 + k, i],
                device_id=device(d), device_id_type=MESH))
        return copies

    pl.semaphore_wait(barrier, len(partners))
    first = state_copies(0)
    for c in first:
        c.start()

    tall[...] = jnp.zeros_like(tall)
    w1 = w1_ref[...] * 0.125
    w1h = high(w1)
    tall[0:48, 0:64] = w1h
    tall[48:96, 0:64] = w1h
    b1 = split3(b1_ref[...])
    for s in range(3):
        tall[96 + s : 97 + s, 0:64] = b1[s]
    tall[112:160, 0:64] = w1 - w1h
    l1[...] = tall[...].T[0:64, 0:P_ROWS].astype(BF16)

    tall[...] = jnp.zeros_like(tall)
    w2 = w2_ref[...]
    w2h = high(w2)
    tall[0:64, 0:16] = w2h
    tall[64:128, 0:16] = w2h
    b2 = split3(b2_ref[...])
    for s in range(3):
        tall[128 + s : 129 + s, 0:16] = b2[s]
    tall[144:208, 0:16] = w2 - w2h
    l2[...] = tall[...].T[0:16, 0:H_ROWS].astype(BF16)

    tall[...] = jnp.zeros_like(tall)
    tall[0:48, 0:64] = -w1
    w1t = tall[...].T[0:64, 0:48]
    tall[...] = jnp.zeros_like(tall)
    w1th = high(w1t)
    tall[0:64, 0:48] = w1th
    tall[64:128, 0:48] = w1th
    tall[128:192, 0:48] = w1t - w1th
    l4[...] = tall[...].T[0:48, 0:192].astype(BF16)

    tall[...] = jnp.zeros_like(tall)
    tall[0:64, 0:16] = w2
    w2t = tall[...].T[0:16, 0:64]
    tall[...] = jnp.zeros_like(tall)
    w2th = high(w2t)
    tall[0:16, 0:64] = w2th
    tall[16:32, 0:64] = w2th
    tall[32:48, 0:64] = w2t - w2th
    l3[...] = tall[...].T[0:64, 0:48].astype(BF16)

    kk = lax.broadcasted_iota(jnp.int32, (128, 128), 0)
    yy = lax.broadcasted_iota(jnp.int32, (128, 128), 1)
    feature = lax.rem(lax.div(kk, 8), 3)
    row8 = lax.rem(kk, 8)
    hit = jnp.logical_and(kk < 72, yy == jnp.where(row8 < 4, 127, 0))
    for x in range(BX):
        for f in range(3):
            sign = jnp.where(row8 < 4, 1.0, -1.0) if f == 1 else 1.0
            onehot[x * 3 + f] = jnp.where(
                jnp.logical_and(hit, jnp.logical_and(feature == f, lax.rem(row8, 4) == x)), sign, 0.0
            ).astype(BF16)
    turn[...] = jnp.zeros_like(turn)
    for k in range(2):
        for x in range(BX):
            percs[k, x, 2 * PERC : 2 * PERC + 16, :] = jnp.ones((16, ROW), BF16)
            hids[k, x, 2 * HID : 2 * HID + 16, :] = jnp.ones((16, ROW), BF16)
    for x in (0, 1, BX + 2, BX + 3):
        zf[x] = jnp.zeros_like(zf[x])
    for x in range(BX):
        for z in range(BZ):
            carried[x, z] = cot_ref[pl.ds(x * BZ + z, CH, stride=BX * BZ), :]

    low_x, top_x = (gx > 0).astype(F32), (gx < nx - 1).astype(F32)
    low_y, top_y = (gy > 0).astype(F32), (gy < ny - 1).astype(F32)
    low_z, top_z = (gz > 0).astype(F32), (gz < nz - 1).astype(F32)
    in_x, in_z = (low_x, 1.0, top_x), (low_z, 1.0, top_z)

    def store_split(ref, lead, rows, value, again):
        hi = value.astype(BF16)
        lo = (value - hi.astype(F32)).astype(BF16)
        ref[(*lead, pl.ds(0, rows))] = hi
        ref[(*lead, pl.ds(rows, rows))] = lo
        ref[(*lead, pl.ds(again, rows))] = hi

    def place(rows24, features):
        parts = split3(rows24)
        n = 8 * features
        for s in range(3):
            turn[24 * s : 24 * s + n, :] = parts[s]
        turned = turn[...].T.astype(BF16)
        for x in range(BX):
            for f in range(features):
                placed[x * 3 + f] = dot(turned, onehot[x * 3 + f])

    def clear_outside(k):
        @pl.when(gx == 0)
        def _():
            field[k, 0] = jnp.zeros_like(field[k, 0])
        @pl.when(gx == nx - 1)
        def _():
            field[k, BX + 1] = jnp.zeros_like(field[k, BX + 1])
        @pl.when(gz == 0)
        def _():
            field[k, :, 0] = jnp.zeros_like(field[k, :, 0])
        @pl.when(gz == nz - 1)
        def _():
            field[k, :, BZ + 1] = jnp.zeros_like(field[k, :, BZ + 1])

    def filter_columns(k):
        grid = {}
        for ix in range(3):
            for iz in range(3):
                tile = jnp.where(sub < 4, halos[k, 1, ix, iz] * top_y, halos[k, 0, ix, iz] * low_y)
                grid[ix, iz] = tile * (in_x[ix] * in_z[iz])
        xs, xd = [], []
        for iz in range(3):
            mid = grid[1, iz]
            after = pltpu.roll(jnp.where(lax.rem(sub, 4) == 0, pltpu.roll(grid[2, iz], 4, 0), mid), 7, 0)
            before = pltpu.roll(jnp.where(lax.rem(sub, 4) == 3, pltpu.roll(grid[0, iz], 4, 0), mid), 1, 0)
            xs.append(before + 2.0 * mid + after)
            xd.append(after - before)

        def around(t):
            above = pltpu.roll(jnp.where(lane < 16, t[2], t[1]), 112, 1)
            below = pltpu.roll(jnp.where(lane >= 112, t[0], t[1]), 16, 1)
            return below, above

        d_below, d_above = around(xd)
        s_below, s_above = around(xs)
        place(jnp.concatenate([
            d_below + 2.0 * xd[1] + d_above,
            s_below + 2.0 * xs[1] + s_above,
            s_above - s_below], axis=0), 3)

    def forward(k):
        def body(x, _):
            zs, zd = [], []
            for i in range(3):
                v = field[k, x + i]
                zs.append(v[0:8] + 2.0 * v[1:9] + v[2:10])
                zd.append(v[2:10] - v[0:8])
            b = zs[2] - zs[0]
            a = zs[0] + 2.0 * zs[1] + zs[2]
            c = zd[0] + 2.0 * zd[1] + zd[2]
            up = lambda t: pltpu.roll(t, 127, 2) * not_last
            down = lambda t: pltpu.roll(t, 1, 2) * not_first
            features = (
                2.0 * b + up(b) + down(b),
                up(a) - down(a),
                2.0 * c + up(c) + down(c),
            )
            for f in range(3):
                perc = features[f] + placed[x * 3 + f].reshape(BZ, CH, BY)
                flat = jnp.concatenate([perc[z] for z in range(BZ)], axis=1)
                hi = flat.astype(BF16)
                lo = (flat - hi.astype(F32)).astype(BF16)
                percs[k, x, f * 16 : f * 16 + 16] = hi
                percs[k, x, 48 + f * 16 : 64 + f * 16] = lo
                percs[k, x, 112 + f * 16 : 128 + f * 16] = hi
            hid = jnp.tanh(dot(l1[...], percs[k, x]))
            hidden[k, x] = hid
            store_split(hids, (k, x), HID, hid, 2 * HID + 16)
            if k == 0:
                update = dot(l2[...], hids[k, x])
                mask = mask_ref[pl.ds(pl.multiple_of(x * BZ, 8), BZ), :].astype(F32)
                for z in range(BZ):
                    field[1, x + 1, z + 1] = field[0, x + 1, z + 1] + mask[z : z + 1] * update[:, z * BY : (z + 1) * BY]
            return 0
        lax.fori_loop(0, BX, body, 0)

    def cells(k):
        def body(x, _):
            mask = mask_ref[pl.ds(pl.multiple_of((k * BX + x) * BZ, 8), BZ), :].astype(F32)
            g = carried[x]
            du = jnp.concatenate([mask[z : z + 1] * g[z] for z in range(BZ)], axis=1)
            store_split(dus, (x,), CH, du, 2 * CH)
            hid = hidden[k, x]
            dz = dot(l3[...], dus[x]) * (1.0 - hid * hid)
            store_split(dzs, (x,), HID, dz, 2 * HID)
            return 0
        lax.fori_loop(0, BX, body, 0)

    def adjoint(k):
        def body(x, _):
            dp = dot(l4[...], dzs[x])
            zero = jnp.zeros((2, CH, BY), F32)
            for f in range(3):
                q = jnp.concatenate(
                    [zero] + [dp[f * 16 : f * 16 + 16, z * BY : (z + 1) * BY].reshape(1, CH, BY) for z in range(BZ)] + [zero], axis=0)
                zf[x + 2, f] = q[2:12] - q[0:10] if f == 2 else q[0:10] + 2.0 * q[1:11] + q[2:12]
            return 0
        lax.fori_loop(0, BX, body, 0)

        def plane_body(xo, _):
            pr = zf[xo + 2, 0] - zf[xo, 0] + zf[xo, 2] + 2.0 * zf[xo + 1, 2] + zf[xo + 2, 2]
            q = zf[xo, 1] + 2.0 * zf[xo + 1, 1] + zf[xo + 2, 1]
            up, down = pr + q, pr - q
            outs[k, xo] = 2.0 * pr + pltpu.roll(down, 1, 2) * not_first + pltpu.roll(up, 127, 2) * not_last
            both = jnp.where(lane3 == 0, up, down)
            main = both[1:9].reshape(128, 128).T
            side = jnp.concatenate([both[0], both[9]], axis=0)
            side = jnp.concatenate([side, jnp.zeros((96, 128), F32)], axis=0).T
            for s, r in ((0, 0), (1, 127)):
                opacks[k, s, 0, pl.ds(xo, 1)] = main[r : r + 1]
                opacks[k, s, 1, pl.ds(xo, 1)] = side[r : r + 1]
            return 0
        lax.fori_loop(0, BX + 2, plane_body, 0)

    def add_halo(k):
        total = jnp.zeros((8, 128), F32)
        for iy in range(2):
            base = 4 if iy == 0 else 0
            in_y = low_y if iy == 0 else top_y
            for ix in range(3):
                part = jnp.zeros((8, 128), F32)
                for iz in range(3):
                    if iz == 1:
                        t = rpacks[k, iy, ix, iz, 0]
                    else:
                        t = pltpu.roll(rpacks[k, iy, ix, iz, 1], 112, 1)
                        t = jnp.where(lane < 16 if iz == 0 else lane >= 112, t, 0.0)
                    part = part + t * (in_y * in_x[ix] * in_z[iz])
                if ix == 1:
                    part = jnp.where(lax.div(sub, 4) == base // 4, pltpu.roll(part, 3 if iy == 0 else 7, 0), 0.0)
                else:
                    row = base if ix == 0 else base + 3
                    part = jnp.where(sub == row, pltpu.roll(part, 7 if iy == 0 else 3, 0), 0.0)
                total = total + part
        place(total, 1)

        def body(x, _):
            carried[x] = carried[x] + outs[k, x + 1, pl.ds(1, BZ)] + placed[x * 3].reshape(BZ, CH, BY)
            return 0
        lax.fori_loop(0, BX, body, 0)
        for ix in range(2):
            x = 0 if ix == 0 else BX - 1
            m = low_x if ix == 0 else top_x
            carried[x] = carried[x] + rx[k, ix] * m
            for iz in range(2):
                z = 0 if iz == 0 else BZ - 1
                carried[x, z] = carried[x, z] + rc[k, ix, iz] * (m * (low_z if iz == 0 else top_z))
        for iz in range(2):
            z = 0 if iz == 0 else BZ - 1
            m = low_z if iz == 0 else top_z
            carried[:, z] = carried[:, z] + rz[k, :, iz] * m

    def weight_grads(k):
        def body(x, acc):
            g1, g2 = acc
            g1 = g1 + dot_nt(percs[k, x, 0:112], dzs[x, 0:128])
            g2 = g2 + dot_nt(dus[x, 0:32], hids[k, x, 0:144])
            return g1, g2
        return lax.fori_loop(0, BX, body, (jnp.zeros((112, 128), F32), jnp.zeros((32, 144), F32)))

    for c in first:
        c.wait_recv()
    clear_outside(0)
    filter_columns(0)
    forward(0)
    pack_state(1)
    second = state_copies(1)
    for c in second:
        c.start()
    for c in second:
        c.wait_recv()
    clear_outside(1)
    filter_columns(1)
    forward(1)
    cells(1)
    adjoint(1)
    third = out_copies(1)
    for c in third:
        c.start()
    ga1, ga2 = weight_grads(1)
    for c in third:
        c.wait_recv()
    add_halo(1)
    cells(0)
    gb1, gb2 = weight_grads(0)
    g1, g2 = ga1 + gb1, ga2 + gb2

    both = g1[0:48] + g1[48:96]
    both = both + pltpu.roll(both, 64, 1)
    bias1 = g1[96:104]
    bias1 = bias1 + pltpu.roll(bias1, 64, 1)
    second_w = g2[0:16] + g2[16:32]
    bias2 = second_w[:, 128:129]
    second_w = second_w[:, 0:128]
    second_w = second_w + pltpu.roll(second_w, 64, 1)
    left = lax.broadcasted_iota(jnp.int32, (16, 128), 1) < 64
    both = both * 0.125
    sums[0:16] = jnp.where(left, both[0:16], second_w)
    sums[16:24] = jnp.where(left[0:8], both[16:24], bias1)
    sums[24:40] = jnp.where(left, both[24:40], jnp.broadcast_to(bias2, (16, 128)))
    sums[40:48] = both[40:48]

    pieces = ny * nz
    rows = 48 // pieces
    for p in range(pieces):
        src1[p, 0:rows] = sums[p * rows : (p + 1) * rows]
    mine = gy * nz + gz

    def member(o):
        _, y, z = device(o)
        return y * nz + z

    stage1 = [pltpu.make_async_remote_copy(
        src_ref=src1.at[member(o)], dst_ref=rx1.at[i],
        send_sem=ar_send.at[0, i], recv_sem=ar_recv.at[0, i],
        device_id=device(o), device_id_type=MESH) for i, o in enumerate(plane)]
    for c in stage1:
        c.start()
    adjoint(0)
    fourth = out_copies(0)
    for c in fourth:
        c.start()
    total = src1[mine]
    for i, c in enumerate(stage1):
        c.wait_recv()
        total = total + rx1[i]
    rx2[gx] = total
    stage2 = [pltpu.make_async_remote_copy(
        src_ref=rx2.at[gx], dst_ref=rx2.at[gx],
        send_sem=ar_send.at[1, i], recv_sem=ar_recv.at[1, i],
        device_id=device(o), device_id_type=MESH) for i, o in enumerate(line)]
    for c in stage2:
        c.start()
    for c in fourth:
        c.wait_recv()
    add_halo(0)
    for x in range(BX):
        for z in range(BZ):
            grad_ref[pl.ds(x * BZ + z, CH, stride=BX * BZ), :] = carried[x, z]
    for c in stage2:
        c.wait_recv()
    for c in stage2:
        c.wait_send()
    total = rx2[0]
    for i in range(1, nx):
        total = total + rx2[i]
    rx3[mine] = total
    stage3 = [pltpu.make_async_remote_copy(
        src_ref=rx3.at[mine], dst_ref=rx3.at[mine],
        send_sem=ar_send.at[2, i], recv_sem=ar_recv.at[2, i],
        device_id=device(o), device_id_type=MESH) for i, o in enumerate(plane)]
    for c in stage3:
        c.start()
    for c in first + second + third + fourth + stage1:
        c.wait_send()
    for c in stage3:
        c.wait_recv()
    for p in range(pieces):
        sums[p * rows : (p + 1) * rows] = rx3[p, 0:rows]
    scale = 1.0 / math.sqrt(nx * BX * ny * BY * nz * BZ)
    final = sums[...] * scale
    gw1_ref[...] = final[:, 0:64]
    gb1_ref[...] = final[16:17, 64:128]
    turn[0:48] = final
    turned = turn[...].T
    gw2_ref[...] = turned[64:128, 0:16]
    gb2_ref[...] = turned[64:65, 24:40]
    for c in stage3:
        c.wait_send()


def body(start_state, cotangent, update_masks, first_weight, first_bias, second_weight, second_bias):
    sizes = (lax.axis_size("gx"), lax.axis_size("gy"), lax.axis_size("gz"))
    pieces = sizes[1] * sizes[2]
    vmem = pl.BlockSpec(memory_space=pltpu.VMEM)
    scratch = [
        pltpu.VMEM((2, BX + 2, BZ + 2, CH, BY), F32),
        pltpu.VMEM((2, 8, 128), F32),
        pltpu.VMEM((2, 2, 3, 3, 8, 128), F32),
        pltpu.VMEM((2, BX + 2, BZ + 2, CH, BY), F32),
        pltpu.VMEM((2, 2, 2, 8, 128), F32),
        pltpu.VMEM((2, 2, BZ, CH, BY), F32),
        pltpu.VMEM((2, BX, 2, CH, BY), F32),
        pltpu.VMEM((2, 2, 2, CH, BY), F32),
        pltpu.VMEM((2, 2, 3, 3, 2, 8, 128), F32),
        pltpu.VMEM((2, BX, P_ROWS, ROW), BF16),
        pltpu.VMEM((2, BX, H_ROWS, ROW), BF16),
        pltpu.VMEM((2, BX, HID, ROW), F32),
        pltpu.VMEM((BX, 3 * HID, ROW), BF16),
        pltpu.VMEM((BX, 3 * CH, ROW), BF16),
        pltpu.VMEM((BX, BZ, CH, BY), F32),
        pltpu.VMEM((BX + 4, 3, BZ + 2, CH, BY), F32),
        pltpu.VMEM((12, 128, 128), F32),
        pltpu.VMEM((12, 128, 128), BF16),
        pltpu.VMEM((256, 128), F32),
        pltpu.VMEM((HID, P_ROWS), BF16),
        pltpu.VMEM((CH, H_ROWS), BF16),
        pltpu.VMEM((HID, 3 * CH), BF16),
        pltpu.VMEM((PERC, 3 * HID), BF16),
        pltpu.VMEM((128, 128), F32),
        pltpu.VMEM((48, 128), F32),
        pltpu.VMEM((pieces, 8, 128), F32),
        pltpu.VMEM((pieces, 8, 128), F32),
        pltpu.VMEM((sizes[0], 8, 128), F32),
        pltpu.VMEM((pieces, 8, 128), F32),
        pltpu.SemaphoreType.DMA((4, 26)),
        pltpu.SemaphoreType.DMA((4, 26)),
        pltpu.SemaphoreType.DMA((3, 16)),
        pltpu.SemaphoreType.DMA((3, 16)),
    ]
    outs = pl.pallas_call(
        functools.partial(kernel, sizes),
        out_shape=(
            jax.ShapeDtypeStruct((CH * BX * BZ, BY), F32),
            jax.ShapeDtypeStruct((PERC, HID), F32),
            jax.ShapeDtypeStruct((1, HID), F32),
            jax.ShapeDtypeStruct((HID, CH), F32),
            jax.ShapeDtypeStruct((1, CH), F32),
        ),
        in_specs=[vmem] * 7,
        out_specs=(vmem,) * 5,
        scratch_shapes=scratch,
        compiler_params=pltpu.CompilerParams(
            collective_id=0, has_side_effects=True, vmem_limit_bytes=40 * 1024 * 1024),
        cost_estimate=pl.CostEstimate(flops=2 * 10**8, bytes_accessed=10**6, transcendentals=524288),
        name="automaton",
    )(
        start_state.reshape(CH * BX * BZ, BY),
        cotangent.reshape(CH * BX * BZ, BY),
        update_masks.reshape(2 * BX * BZ, BY),
        first_weight, first_bias.reshape(1, HID), second_weight, second_bias.reshape(1, CH),
    )
    grad, gw1, gb1, gw2, gb2 = outs
    return grad.reshape(CH, BX, BZ, BY), gw1, gb1.reshape(HID), gw2, gb2.reshape(CH)


def solution(mesh):
    grid = P(None, "gx", "gz", "gy")
    return jax.shard_map(
        body, mesh=mesh,
        in_specs=(grid, grid, grid, P(), P(), P(), P()),
        out_specs=(grid, P(), P(), P(), P()),
        check_vma=False)
```

time: 240 us -> 63.3 us (0.26); the launches traced: 237 us -> 63 us
  blocking collectives: 79.9 us -> 0 us
  starting transfers between devices: 68.3 us -> 0 us
  Pallas kernels: 0 us -> 55.4 us
  waiting for transfers between devices: 50.8 us -> 0 us
  other arithmetic: 13.3 us -> 0 us
  matrix products: 11 us -> 0 us
  local copies, waits for them, and re-layouts: 12.3 us -> 6.99 us
    psum x1 -> x0, blocking collectives: 79.9 us -> none  [body(): lax.psum((totals[0], totals[1], totals[2], totals[3]), ('gx', 'gy', 'gz'))]
    ppermute x24 -> x0, starting transfers between devices: 68.3 us -> none  [the longest x12 50.1 us: extended(): before = lax.ppermute(last, axis, up)]
    pallas_call x0 -> x1, Pallas kernels: none -> 55.4 us  [body(): pl.pallas_call(functools.partial(kernel, sizes), out_shape=(jax.ShapeDtyp...]
    ppermute x24 -> x0, waiting for transfers between devices: 50.8 us -> none  [the longest x12 31.4 us: extended(): after = lax.ppermute(initial, axis, down)]
    dot_general x11 -> x0, matrix products: 11 us -> none  [the longest x2 2.54 us: backward_cells(): jnp.einsum('ho,oxzy->hxzy', second_weight, masked, precision=highest)]
    sub x12 -> x0, other arithmetic: 4.9 us -> none  [differ(): return shifted(field, axis, 2) - shifted(field, axis, 0)]
    slice x12 -> x0, local copies, waits for them, and re-layouts: 3.81 us -> none  [the longest x9 2.06 us: extended(): last = lax.slice_in_dim(value, length - width, length, axis=dim)]
    concatenate x9 -> x0, other arithmetic: 3.47 us -> none  [extended(): value = jnp.concatenate([before, value, after], axis=dim)]
  transfers between devices with their start and end apart: 24 -> 0, of which waited for: 19 -> 0; matrix products, arithmetic and copies ran while one was open for 2% -> 0% of each run, Pallas kernels for 0% -> 0%
where the time goes in v1:
time: 63.3 us; the launch traced here: 63 us
  Pallas kernels  55.4 us (88%)
  local copies, waits for them, and re-layouts  6.99 us (11%)
  between operations  0.67 us (1%)
    pallas_call x1, Pallas kernels, body(): pl.pallas_call(functools.partial(kernel, sizes), out_shape=(jax.ShapeDtyp...  55.4 us
    unnamed x20, local copies, waits for them, and re-layouts  6.99 us

profile of v1, /device:TPU:1, one launch (start us, length us, event | category | flops | bytes accessed | tf_op | source)
XLA Modules:
  0.0 63.0 jit_solution(2547357365991695529)
XLA Ops:
  0.6 0.0 copy-start.6
  0.6 0.0 copy-start.2
  0.7 0.7 %copy-done.6 = f32[64,16]{0,1:T(8,128)S(1)} copy-done((f32[64,16]{0,1:T(8,128)S(1)}, f32[64,16]{0,1:T(8,128)}, u32[]{:S(2)}) %copy-start.6) | copy-done | bytes 4120
  1.3 0.0 copy-start.4
  1.3 0.0 copy-start.5
  1.3 0.1 copy.12.w2_ref
  1.4 0.0 copy-done.2
  1.4 0.6 copy-done.4
  2.0 0.0 copy-done.5
  2.0 0.0 copy-start
  2.0 0.9 %copy-done = f32[16,4,8,128]{3,2,1,0:T(8,128)S(1)} copy-done((f32[16,4,8,128]{3,2,1,0:T(8,128)S(1)}, f32[16,4,8,128]{3,2,1,0:T(8,128)}, u32[]{:S(2)}) %copy-start) | copy-done | bytes 262168
  3.0 0.0 copy-start.1
  3.0 0.9 %copy-done.1 = f32[16,4,8,128]{3,2,1,0:T(8,128)S(1)} copy-done((f32[16,4,8,128]{3,2,1,0:T(8,128)S(1)}, f32[16,4,8,128]{3,2,1,0:T(8,128)}, u32[]{:S(2)}) %copy-start.1) | copy-done | bytes 262168
  3.9 0.0 copy-start.3
  3.9 0.7 %copy-done.3 = f32[48,64]{1,0:T(8,128)S(1)} copy-done((f32[48,64]{1,0:T(8,128)S(1)}, f32[48,64]{1,0:T(8,128)}, u32[]{:S(2)}) %copy-start.3) | copy-done | bytes 12312
  4.6 55.4 %automaton.1 = (f32[512,128]{1,0:T(8,128)S(1)}, f32[48,64]{1,0:T(8,128)S(1)}, f32[1,64]{1,0:T(1,128)S(1)}, f32[64,16]{1,0:T(8,128)S(1)}, f32[1,16]{1,0:T(1,128)S(1)}) custom-call(f32[512,128]{1,0:T(8,128)S(1)} %bitcast.9, f32[512,128]{1,0:T(8,128)S(1)} %bitcast.10, s32[64,128]{1,0:T(8,128)S(1)} %bitcast.11, f32[48,64]{1,0:T(8,128)S(1)} %copy-done.3, ...), custom_call_target="tpu_custom_call" | custom-call | flops 200000000 | bytes 1000000 | tf_op jit(solution)/shard_map/automaton/pallas_call | solution.py:548
  60.0 0.7 %copy.13 = f32[64,16]{0,1:T(8,128)} copy(f32[64,16]{1,0:T(8,128)S(1)} %get-tuple-element.18) | data formatting | bytes 8192
  60.7 0.7 %copy.18 = f32[16,4,8,128]{3,2,1,0:T(8,128)} copy(f32[16,4,8,128]{3,2,1,0:T(8,128)S(1)} %bitcast.8) | data formatting | bytes 524288
  61.4 0.6 copy.19
  62.0 0.5 copy.20
  62.5 0.5 copy.21
Async XLA Ops:
  0.6 0.7 %copy-start.6 = (f32[64,16]{0,1:T(8,128)S(1)}, f32[64,16]{0,1:T(8,128)}, u32[]{:S(2)}) copy-start(f32[64,16]{0,1:T(8,128)} %param.12) | copy-start | bytes 12292
  0.6 0.8 %copy-start.2 = (s32[2,4,8,128]{3,2,1,0:T(8,128)S(1)}, s32[2,4,8,128]{3,2,1,0:T(8,128)}, u32[]{:S(2)}) copy-start(s32[2,4,8,128]{3,2,1,0:T(8,128)} %param.9) | copy-start | bytes 98308
  1.3 0.7 %copy-start.4 = (f32[64]{0:T(128)S(1)}, f32[64]{0:T(128)}, u32[]{:S(2)}) copy-start(f32[64]{0:T(128)} %param.11) | copy-start | bytes 772
  1.3 0.7 %copy-start.5 = (f32[16]{0:T(128)S(1)}, f32[16]{0:T(128)}, u32[]{:S(2)}) copy-start(f32[16]{0:T(128)} %param.13) | copy-start | bytes 196
  2.0 0.9 %copy-start = (f32[16,4,8,128]{3,2,1,0:T(8,128)S(1)}, f32[16,4,8,128]{3,2,1,0:T(8,128)}, u32[]{:S(2)}) copy-start(f32[16,4,8,128]{3,2,1,0:T(8,128)} %param.7) | copy-start | bytes 786436
  3.0 0.9 %copy-start.1 = (f32[16,4,8,128]{3,2,1,0:T(8,128)S(1)}, f32[16,4,8,128]{3,2,1,0:T(8,128)}, u32[]{:S(2)}) copy-start(f32[16,4,8,128]{3,2,1,0:T(8,128)} %param.8) | copy-start | bytes 786436
  3.9 0.7 %copy-start.3 = (f32[48,64]{1,0:T(8,128)S(1)}, f32[48,64]{1,0:T(8,128)}, u32[]{:S(2)}) copy-start(f32[48,64]{1,0:T(8,128)} %w1_ref.1) | copy-start | bytes 36868

commit v2 on v1

--- a/solution.py
+++ b/solution.py
@@ -23,6 +23,9 @@
 FLAT = [d for d in DIRS if d[1] == 0]
 TALL = [d for d in DIRS if d[1] != 0]
 
+FORTH = 2 * BZ * CH + 2 * BX * CH + 4 * CH + 18 * 8
+BACK = 2 * BZ * CH + 2 * BX * CH + 4 * CH + 18 * 16
+
 
 def high(value):
     return value.astype(BF16).astype(F32)
@@ -52,14 +55,20 @@
 
 def kernel(
     sizes,
+    state_in, cot_in, mask_in, w1_in, b1_in, w2_in, b2_in,
+    grad_out, gw1_out, gb1_out, gw2_out, gb2_out,
+    grad_ref, gw1_ref, gb1_ref, gw2_ref, gb2_ref,
     state_ref, cot_ref, mask_ref, w1_ref, b1_ref, w2_ref, b2_ref,
-    grad_ref, gw1_ref, gb1_ref, gw2_ref, gb2_ref,
     field, packs, halos, outs, opacks, rx, rz, rc, rpacks,
-    percs, hids, hidden, dzs, dus, carried, zf, placed, onehot,
+    percs, hids, hidden, grads, carried, zf, placed, onehot,
     tall, l1, l2, l3, l4, turn, sums, src1, rx1, rx2, rx3,
-    send_sem, recv_sem, ar_send, ar_recv,
+    tally, load_sem, store_sem, send_sem, recv_sem, ar_send, ar_recv,
 ):
     nx, ny, nz = sizes
+    loads = [pltpu.make_async_copy(a, b, load_sem.at[i]) for i, (a, b) in enumerate((
+        (state_in, state_ref), (w1_in, w1_ref), (b1_in, b1_ref), (w2_in, w2_ref), (b2_in, b2_ref), (cot_in, cot_ref), (mask_in, mask_ref)))]
+    for c in loads:
+        c.start()
     gx, gy, gz = lax.axis_index("gx"), lax.axis_index("gy"), lax.axis_index("gz")
 
     def device(offset):
@@ -87,6 +96,9 @@
     lane3 = lax.broadcasted_iota(jnp.int32, (1, 1, 128), 2)
     not_first = (lane3 > 0).astype(F32)
     not_last = (lane3 < 127).astype(F32)
+
+    def wait_rows(rows, sem):
+        pltpu.make_async_copy(tally.at[pl.ds(0, rows)], tally.at[pl.ds(0, rows)], sem).wait()
 
     def pack_state(k):
         def body(x, _):
@@ -97,6 +109,7 @@
             return 0
         lax.fori_loop(0, BX, body, 0)
 
+    loads[0].wait()
     for x in range(BX):
         for z in range(BZ):
             field[0, x + 1, z + 1] = state_ref[pl.ds(x * BZ + z, CH, stride=BX * BZ), :]
@@ -105,25 +118,22 @@
     def state_copies(k):
         copies = []
         for d in FLAT:
-            i = DIRS.index(d)
             copies.append(pltpu.make_async_remote_copy(
                 src_ref=field.at[k, span(d[0], BX, "own"), span(d[2], BZ, "own")],
                 dst_ref=field.at[k, span(-d[0], BX, "halo"), span(-d[2], BZ, "halo")],
-                send_sem=send_sem.at[k, i], recv_sem=recv_sem.at[k, i],
+                send_sem=send_sem.at[k], recv_sem=recv_sem.at[k],
                 device_id=device(d), device_id_type=MESH))
         for d in TALL:
-            i = DIRS.index(d)
             copies.append(pltpu.make_async_remote_copy(
                 src_ref=packs.at[k],
                 dst_ref=halos.at[k, 0 if d[1] > 0 else 1, 1 - d[0], 1 - d[2]],
-                send_sem=send_sem.at[k, i], recv_sem=recv_sem.at[k, i],
+                send_sem=send_sem.at[k], recv_sem=recv_sem.at[k],
                 device_id=device(d), device_id_type=MESH))
         return copies
 
     def out_copies(k):
         copies = []
         for d in FLAT:
-            i = DIRS.index(d)
             if d[0] and d[2]:
                 dst = rc.at[k, pl.ds(0 if d[0] > 0 else 1, 1), pl.ds(0 if d[2] > 0 else 1, 1)]
             elif d[0]:
@@ -133,14 +143,13 @@
             copies.append(pltpu.make_async_remote_copy(
                 src_ref=outs.at[k, span(d[0], BX, "halo"), span(d[2], BZ, "halo")],
                 dst_ref=dst,
-                send_sem=send_sem.at[2 + k, i], recv_sem=recv_sem.at[2 + k, i],
+                send_sem=send_sem.at[2 + k], recv_sem=recv_sem.at[2 + k],
                 device_id=device(d), device_id_type=MESH))
         for d in TALL:
-            i = DIRS.index(d)
             copies.append(pltpu.make_async_remote_copy(
                 src_ref=opacks.at[k, 0 if d[1] < 0 else 1],
                 dst_ref=rpacks.at[k, 0 if d[1] > 0 else 1, 1 - d[0], 1 - d[2]],
-                send_sem=send_sem.at[2 + k, i], recv_sem=recv_sem.at[2 + k, i],
+                send_sem=send_sem.at[2 + k], recv_sem=recv_sem.at[2 + k],
                 device_id=device(d), device_id_type=MESH))
         return copies
 
@@ -149,6 +158,8 @@
     for c in first:
         c.start()
 
+    for c in loads[1:5]:
+        c.wait()
     tall[...] = jnp.zeros_like(tall)
     w1 = w1_ref[...] * 0.125
     w1h = high(w1)
@@ -161,7 +172,10 @@
     l1[...] = tall[...].T[0:64, 0:P_ROWS].astype(BF16)
 
     tall[...] = jnp.zeros_like(tall)
-    w2 = w2_ref[...]
+    w2t = w2_ref[...]
+    tall[0:16, 0:64] = w2t
+    w2 = tall[...].T[0:64, 0:16]
+    tall[...] = jnp.zeros_like(tall)
     w2h = high(w2)
     tall[0:64, 0:16] = w2h
     tall[64:128, 0:16] = w2h
@@ -176,14 +190,11 @@
     w1t = tall[...].T[0:64, 0:48]
     tall[...] = jnp.zeros_like(tall)
     w1th = high(w1t)
-    tall[0:64, 0:48] = w1th
+    tall[0:64, 0:48] = w1t - w1th
     tall[64:128, 0:48] = w1th
-    tall[128:192, 0:48] = w1t - w1th
+    tall[128:192, 0:48] = w1th
     l4[...] = tall[...].T[0:48, 0:192].astype(BF16)
 
-    tall[...] = jnp.zeros_like(tall)
-    tall[0:64, 0:16] = w2
-    w2t = tall[...].T[0:16, 0:64]
     tall[...] = jnp.zeros_like(tall)
     w2th = high(w2t)
     tall[0:16, 0:64] = w2th
@@ -209,6 +220,8 @@
             hids[k, x, 2 * HID : 2 * HID + 16, :] = jnp.ones((16, ROW), BF16)
     for x in (0, 1, BX + 2, BX + 3):
         zf[x] = jnp.zeros_like(zf[x])
+    for c in loads[5:]:
+        c.wait()
     for x in range(BX):
         for z in range(BZ):
             carried[x, z] = cot_ref[pl.ds(x * BZ + z, CH, stride=BX * BZ), :]
@@ -218,12 +231,9 @@
     low_z, top_z = (gz > 0).astype(F32), (gz < nz - 1).astype(F32)
     in_x, in_z = (low_x, 1.0, top_x), (low_z, 1.0, top_z)
 
-    def store_split(ref, lead, rows, value, again):
+    def halves(value):
         hi = value.astype(BF16)
-        lo = (value - hi.astype(F32)).astype(BF16)
-        ref[(*lead, pl.ds(0, rows))] = hi
-        ref[(*lead, pl.ds(rows, rows))] = lo
-        ref[(*lead, pl.ds(again, rows))] = hi
+        return hi, (value - hi.astype(F32)).astype(BF16)
 
     def place(rows24, features):
         parts = split3(rows24)
@@ -295,14 +305,16 @@
             for f in range(3):
                 perc = features[f] + placed[x * 3 + f].reshape(BZ, CH, BY)
                 flat = jnp.concatenate([perc[z] for z in range(BZ)], axis=1)
-                hi = flat.astype(BF16)
-                lo = (flat - hi.astype(F32)).astype(BF16)
+                hi, lo = halves(flat)
                 percs[k, x, f * 16 : f * 16 + 16] = hi
                 percs[k, x, 48 + f * 16 : 64 + f * 16] = lo
                 percs[k, x, 112 + f * 16 : 128 + f * 16] = hi
             hid = jnp.tanh(dot(l1[...], percs[k, x]))
             hidden[k, x] = hid
-            store_split(hids, (k, x), HID, hid, 2 * HID + 16)
+            hi, lo = halves(hid)
+            hids[k, x, 0:64] = hi
+            hids[k, x, 64:128] = lo
+            hids[k, x, 144:208] = hi
             if k == 0:
                 update = dot(l2[...], hids[k, x])
                 mask = mask_ref[pl.ds(pl.multiple_of(x * BZ, 8), BZ), :].astype(F32)
@@ -316,16 +328,22 @@
             mask = mask_ref[pl.ds(pl.multiple_of((k * BX + x) * BZ, 8), BZ), :].astype(F32)
             g = carried[x]
             du = jnp.concatenate([mask[z : z + 1] * g[z] for z in range(BZ)], axis=1)
-            store_split(dus, (x,), CH, du, 2 * CH)
+            hi, lo = halves(du)
+            grads[x, 192:208] = hi
+            grads[x, 208:224] = lo
+            grads[x, 224:240] = hi
             hid = hidden[k, x]
-            dz = dot(l3[...], dus[x]) * (1.0 - hid * hid)
-            store_split(dzs, (x,), HID, dz, 2 * HID)
+            dz = dot(l3[...], grads[x, 192:240]) * (1.0 - hid * hid)
+            hi, lo = halves(dz)
+            grads[x, 0:64] = hi
+            grads[x, 64:128] = hi
+            grads[x, 128:192] = lo
             return 0
         lax.fori_loop(0, BX, body, 0)
 
     def adjoint(k):
         def body(x, _):
-            dp = dot(l4[...], dzs[x])
+            dp = dot(l4[...], grads[x, 0:192])
             zero = jnp.zeros((2, CH, BY), F32)
             for f in range(3):
                 q = jnp.concatenate(
@@ -390,52 +408,48 @@
     def weight_grads(k):
         def body(x, acc):
             g1, g2 = acc
-            g1 = g1 + dot_nt(percs[k, x, 0:112], dzs[x, 0:128])
-            g2 = g2 + dot_nt(dus[x, 0:32], hids[k, x, 0:144])
+            g1 = g1 + dot_nt(percs[k, x, 0:112], grads[x, 64:224])
+            g2 = g2 + dot_nt(grads[x, 192:224], hids[k, x, 0:128])
             return g1, g2
-        return lax.fori_loop(0, BX, body, (jnp.zeros((112, 128), F32), jnp.zeros((32, 144), F32)))
-
-    for c in first:
-        c.wait_recv()
+        return lax.fori_loop(0, BX, body, (jnp.zeros((112, 160), F32), jnp.zeros((32, 128), F32)))
+
+    wait_rows(FORTH, recv_sem.at[0])
     clear_outside(0)
     filter_columns(0)
     forward(0)
     pack_state(1)
-    second = state_copies(1)
-    for c in second:
-        c.start()
-    for c in second:
-        c.wait_recv()
+    for c in state_copies(1):
+        c.start()
+    wait_rows(FORTH, send_sem.at[0])
+    wait_rows(FORTH, recv_sem.at[1])
     clear_outside(1)
     filter_columns(1)
     forward(1)
     cells(1)
     adjoint(1)
-    third = out_copies(1)
-    for c in third:
+    for c in out_copies(1):
         c.start()
     ga1, ga2 = weight_grads(1)
-    for c in third:
-        c.wait_recv()
+    wait_rows(FORTH, send_sem.at[1])
+    wait_rows(BACK, recv_sem.at[3])
     add_halo(1)
     cells(0)
     gb1, gb2 = weight_grads(0)
     g1, g2 = ga1 + gb1, ga2 + gb2
 
-    both = g1[0:48] + g1[48:96]
-    both = both + pltpu.roll(both, 64, 1)
-    bias1 = g1[96:104]
+    both = (g1[0:48] + g1[48:96])[:, 0:128]
+    both = (both + pltpu.roll(both, 64, 1)) * 0.125
+    bias1 = g1[96:104, 0:128]
     bias1 = bias1 + pltpu.roll(bias1, 64, 1)
+    bias2 = jnp.concatenate([g1[96:104, 128:160], jnp.zeros((8, 96), F32)], axis=1)
+    bias2 = pltpu.roll(bias2, 64, 1) + pltpu.roll(bias2, 48, 1)
     second_w = g2[0:16] + g2[16:32]
-    bias2 = second_w[:, 128:129]
-    second_w = second_w[:, 0:128]
     second_w = second_w + pltpu.roll(second_w, 64, 1)
     left = lax.broadcasted_iota(jnp.int32, (16, 128), 1) < 64
-    both = both * 0.125
     sums[0:16] = jnp.where(left, both[0:16], second_w)
     sums[16:24] = jnp.where(left[0:8], both[16:24], bias1)
-    sums[24:40] = jnp.where(left, both[24:40], jnp.broadcast_to(bias2, (16, 128)))
-    sums[40:48] = both[40:48]
+    sums[24:32] = jnp.where(left[0:8], both[24:32], bias2)
+    sums[32:48] = both[32:48]
 
     pieces = ny * nz
     rows = 48 // pieces
@@ -449,68 +463,91 @@
 
     stage1 = [pltpu.make_async_remote_copy(
         src_ref=src1.at[member(o)], dst_ref=rx1.at[i],
-        send_sem=ar_send.at[0, i], recv_sem=ar_recv.at[0, i],
+        send_sem=ar_send.at[0], recv_sem=ar_recv.at[0],
         device_id=device(o), device_id_type=MESH) for i, o in enumerate(plane)]
     for c in stage1:
         c.start()
     adjoint(0)
-    fourth = out_copies(0)
-    for c in fourth:
-        c.start()
+    for c in out_copies(0):
+        c.start()
+    wait_rows(8 * len(plane), ar_recv.at[0])
     total = src1[mine]
-    for i, c in enumerate(stage1):
-        c.wait_recv()
+    for i in range(len(plane)):
         total = total + rx1[i]
     rx2[gx] = total
     stage2 = [pltpu.make_async_remote_copy(
         src_ref=rx2.at[gx], dst_ref=rx2.at[gx],
-        send_sem=ar_send.at[1, i], recv_sem=ar_recv.at[1, i],
-        device_id=device(o), device_id_type=MESH) for i, o in enumerate(line)]
+        send_sem=ar_send.at[1], recv_sem=ar_recv.at[1],
+        device_id=device(o), device_id_type=MESH) for o in line]
     for c in stage2:
         c.start()
-    for c in fourth:
-        c.wait_recv()
+    wait_rows(BACK, send_sem.at[3])
+    wait_rows(8 * len(plane), ar_send.at[0])
+    wait_rows(BACK, recv_sem.at[2])
     add_halo(0)
     for x in range(BX):
         for z in range(BZ):
             grad_ref[pl.ds(x * BZ + z, CH, stride=BX * BZ), :] = carried[x, z]
-    for c in stage2:
-        c.wait_recv()
-    for c in stage2:
-        c.wait_send()
+    stores = [pltpu.make_async_copy(a, b, store_sem.at[i]) for i, (a, b) in enumerate((
+        (grad_ref, grad_out), (gw1_ref, gw1_out), (gb1_ref, gb1_out), (gw2_ref, gw2_out), (gb2_ref, gb2_out)))]
+    stores[0].start()
+    wait_rows(8 * len(line), ar_recv.at[1])
+    wait_rows(8 * len(line), ar_send.at[1])
     total = rx2[0]
     for i in range(1, nx):
         total = total + rx2[i]
     rx3[mine] = total
     stage3 = [pltpu.make_async_remote_copy(
         src_ref=rx3.at[mine], dst_ref=rx3.at[mine],
-        send_sem=ar_send.at[2, i], recv_sem=ar_recv.at[2, i],
-        device_id=device(o), device_id_type=MESH) for i, o in enumerate(plane)]
+        send_sem=ar_send.at[2], recv_sem=ar_recv.at[2],
+        device_id=device(o), device_id_type=MESH) for o in plane]
     for c in stage3:
         c.start()
-    for c in first + second + third + fourth + stage1:
-        c.wait_send()
-    for c in stage3:
-        c.wait_recv()
+    wait_rows(BACK, send_sem.at[2])
+    wait_rows(8 * len(plane), ar_send.at[2])
+    wait_rows(8 * len(plane), ar_recv.at[2])
     for p in range(pieces):
         sums[p * rows : (p + 1) * rows] = rx3[p, 0:rows]
     scale = 1.0 / math.sqrt(nx * BX * ny * BY * nz * BZ)
     final = sums[...] * scale
     gw1_ref[...] = final[:, 0:64]
     gb1_ref[...] = final[16:17, 64:128]
-    turn[0:48] = final
-    turned = turn[...].T
-    gw2_ref[...] = turned[64:128, 0:16]
-    gb2_ref[...] = turned[64:65, 24:40]
-    for c in stage3:
-        c.wait_send()
+    gw2_ref[...] = final[0:16, 64:128]
+    gb2_ref[...] = final[24:25, 64:80]
+    for c in stores[1:]:
+        c.start()
+    for c in stores:
+        c.wait()
+
+
+def write_out(*refs):
+    sems = refs[-1]
+    copies = [pltpu.make_async_copy(refs[i], refs[5 + i], sems.at[i]) for i in range(5)]
+    for c in copies:
+        c.start()
+    for c in copies:
+        c.wait()
 
 
 def body(start_state, cotangent, update_masks, first_weight, first_bias, second_weight, second_bias):
     sizes = (lax.axis_size("gx"), lax.axis_size("gy"), lax.axis_size("gz"))
     pieces = sizes[1] * sizes[2]
-    vmem = pl.BlockSpec(memory_space=pltpu.VMEM)
+    hbm = pl.BlockSpec(memory_space=pltpu.HBM)
+    shapes = ((CH * BX * BZ, BY), (PERC, HID), (1, HID), (CH, HID), (1, CH))
+    shapes = tuple(jax.ShapeDtypeStruct(s, F32) for s in shapes)
     scratch = [
+        pltpu.VMEM((CH * BX * BZ, BY), F32),
+        pltpu.VMEM((PERC, HID), F32),
+        pltpu.VMEM((1, HID), F32),
+        pltpu.VMEM((CH, HID), F32),
+        pltpu.VMEM((1, CH), F32),
+        pltpu.VMEM((CH * BX * BZ, BY), F32),
+        pltpu.VMEM((CH * BX * BZ, BY), F32),
+        pltpu.VMEM((2 * BX * BZ, BY), jnp.int32),
+        pltpu.VMEM((PERC, HID), F32),
+        pltpu.VMEM((1, HID), F32),
+        pltpu.VMEM((CH, HID), F32),
+        pltpu.VMEM((1, CH), F32),
         pltpu.VMEM((2, BX + 2, BZ + 2, CH, BY), F32),
         pltpu.VMEM((2, 8, 128), F32),
         pltpu.VMEM((2, 2, 3, 3, 8, 128), F32),
@@ -523,8 +560,7 @@
         pltpu.VMEM((2, BX, P_ROWS, ROW), BF16),
         pltpu.VMEM((2, BX, H_ROWS, ROW), BF16),
         pltpu.VMEM((2, BX, HID, ROW), F32),
-        pltpu.VMEM((BX, 3 * HID, ROW), BF16),
-        pltpu.VMEM((BX, 3 * CH, ROW), BF16),
+        pltpu.VMEM((BX, 3 * HID + 3 * CH, ROW), BF16),
         pltpu.VMEM((BX, BZ, CH, BY), F32),
         pltpu.VMEM((BX + 4, 3, BZ + 2, CH, BY), F32),
         pltpu.VMEM((12, 128, 128), F32),
@@ -540,35 +576,40 @@
         pltpu.VMEM((pieces, 8, 128), F32),
         pltpu.VMEM((sizes[0], 8, 128), F32),
         pltpu.VMEM((pieces, 8, 128), F32),
-        pltpu.SemaphoreType.DMA((4, 26)),
-        pltpu.SemaphoreType.DMA((4, 26)),
-        pltpu.SemaphoreType.DMA((3, 16)),
-        pltpu.SemaphoreType.DMA((3, 16)),
+        pltpu.VMEM((BACK, 128), F32),
+        pltpu.SemaphoreType.DMA((7,)),
+        pltpu.SemaphoreType.DMA((5,)),
+        pltpu.SemaphoreType.DMA((4,)),
+        pltpu.SemaphoreType.DMA((4,)),
+        pltpu.SemaphoreType.DMA((3,)),
+        pltpu.SemaphoreType.DMA((3,)),
     ]
     outs = pl.pallas_call(
         functools.partial(kernel, sizes),
-        out_shape=(
-            jax.ShapeDtypeStruct((CH * BX * BZ, BY), F32),
-            jax.ShapeDtypeStruct((PERC, HID), F32),
-            jax.ShapeDtypeStruct((1, HID), F32),
-            jax.ShapeDtypeStruct((HID, CH), F32),
-            jax.ShapeDtypeStruct((1, CH), F32),
-        ),
-        in_specs=[vmem] * 7,
-        out_specs=(vmem,) * 5,
+        out_shape=shapes,
+        in_specs=[hbm] * 7,
+        out_specs=(hbm,) * 5,
         scratch_shapes=scratch,
         compiler_params=pltpu.CompilerParams(
-            collective_id=0, has_side_effects=True, vmem_limit_bytes=40 * 1024 * 1024),
+            collective_id=0, has_side_effects=True, vmem_limit_bytes=60 * 1024 * 1024),
         cost_estimate=pl.CostEstimate(flops=2 * 10**8, bytes_accessed=10**6, transcendentals=524288),
         name="automaton",
     )(
         start_state.reshape(CH * BX * BZ, BY),
         cotangent.reshape(CH * BX * BZ, BY),
         update_masks.reshape(2 * BX * BZ, BY),
-        first_weight, first_bias.reshape(1, HID), second_weight, second_bias.reshape(1, CH),
+        first_weight, first_bias.reshape(1, HID), second_weight.T, second_bias.reshape(1, CH),
     )
-    grad, gw1, gb1, gw2, gb2 = outs
-    return grad.reshape(CH, BX, BZ, BY), gw1, gb1.reshape(HID), gw2, gb2.reshape(CH)
+    grad, gw1, gb1, gw2, gb2 = pl.pallas_call(
+        write_out,
+        out_shape=shapes,
+        in_specs=[pl.BlockSpec(memory_space=pltpu.VMEM)] * 5,
+        out_specs=(hbm,) * 5,
+        scratch_shapes=[pltpu.SemaphoreType.DMA((5,))],
+        cost_estimate=pl.CostEstimate(flops=0, bytes_accessed=600000, transcendentals=0),
+        name="write_out",
+    )(*outs)
+    return grad.reshape(CH, BX, BZ, BY), gw1, gb1.reshape(HID), gw2.T, gb2.reshape(CH)
 
 
 def solution(mesh):

time: 63.3 us -> 56.2 us (0.89)
  local copies, waits for them, and re-layouts: 6.99 us -> 0 us
    unnamed x20 -> x0, local copies, waits for them, and re-layouts: 6.99 us -> none
    pallas_call x1 -> x2, Pallas kernels: 55.4 us -> 55.4 us  [the longest x1 53.7 us: body(): pl.pallas_call(functools.partial(kernel, sizes), out_shape=shapes, in_spe...]
where the time goes in v2:
time: 56.2 us; the launch traced here: 56 us
  Pallas kernels  55.4 us (99%)
  between operations  0.64 us (1%)
    pallas_call x1, Pallas kernels, body(): pl.pallas_call(functools.partial(kernel, sizes), out_shape=shapes, in_spe...  53.7 us
    pallas_call x1, Pallas kernels, body(): pl.pallas_call(write_out, out_shape=shapes, in_specs=[pl.BlockSpec(memory...  1.74 us

profile of v2, /device:TPU:1, one launch (start us, length us, event | category | flops | bytes accessed | tf_op | source)
XLA Modules:
  0.0 56.0 jit_solution(14487502519579129586)
XLA Ops:
  0.6 53.7 %automaton.1 = (f32[512,128]{1,0:T(8,128)}, f32[48,64]{1,0:T(8,128)}, f32[1,64]{1,0:T(1,128)}, f32[16,64]{1,0:T(8,128)}, f32[1,16]{1,0:T(1,128)}) custom-call(f32[512,128]{1,0:T(8,128)} %bitcast.10, f32[512,128]{1,0:T(8,128)} %bitcast.11, s32[64,128]{1,0:T(8,128)} %bitcast.13, f32[48,64]{1,0:T(8,128)} %w1_in.1, f32[1,64]{1,0:T(1,128)} %bitcast.16, ...), custom_call_target="tpu_custom_call" | custom-call | flops 200000000 | bytes 1000000 | tf_op jit(solution)/shard_map/automaton/pallas_call | solution.py:587
  54.3 1.7 %write_out.1 = (f32[512,128]{1,0:T(8,128)}, f32[48,64]{1,0:T(8,128)}, f32[1,64]{1,0:T(1,128)}, f32[16,64]{1,0:T(8,128)}, f32[1,16]{1,0:T(1,128)}) custom-call(f32[512,128]{1,0:T(8,128)} %get-tuple-element.15.refs_0_, f32[48,64]{1,0:T(8,128)} %get-tuple-element.16.refs_1_, f32[1,64]{1,0:T(1,128)} %get-tuple-element.17.refs_2_, ...), custom_call_target="tpu_custom_call" | custom-call | bytes 600000 | tf_op jit(solution)/shard_map/write_out/pallas_call | solution.py:603

commit v3 on v2

--- a/solution.py
+++ b/solution.py
@@ -20,8 +20,7 @@
 H_ROWS = 2 * HID + 16 + HID
 
 DIRS = [(dx, dy, dz) for dx in (-1, 0, 1) for dy in (-1, 0, 1) for dz in (-1, 0, 1) if (dx, dy, dz) != (0, 0, 0)]
-FLAT = [d for d in DIRS if d[1] == 0]
-TALL = [d for d in DIRS if d[1] != 0]
+DIRS = sorted(DIRS, key=lambda d: -sum(map(abs, d)))
 
 FORTH = 2 * BZ * CH + 2 * BX * CH + 4 * CH + 18 * 8
 BACK = 2 * BZ * CH + 2 * BX * CH + 4 * CH + 18 * 16
@@ -61,7 +60,7 @@
     state_ref, cot_ref, mask_ref, w1_ref, b1_ref, w2_ref, b2_ref,
     field, packs, halos, outs, opacks, rx, rz, rc, rpacks,
     percs, hids, hidden, grads, carried, zf, placed, onehot,
-    tall, l1, l2, l3, l4, turn, sums, src1, rx1, rx2, rx3,
+    tall, l1, l2, l3, l4, turn, sums, rx0, rx1, rx2, whole,
     tally, load_sem, store_sem, send_sem, recv_sem, ar_send, ar_recv,
 ):
     nx, ny, nz = sizes
@@ -79,13 +78,18 @@
             lax.rem(gz + (oz % nz), nz) if oz % nz else gz,
         )
 
-    plane = [(0, a, b) for a in range(ny) for b in range(nz) if (a, b) != (0, 0)]
-    line = [(a, 0, 0) for a in range(1, nx)]
+    def far(o):
+        return -sum(min(a, n - a) for a, n in zip(o, sizes))
+
+    plane = sorted(((0, a, b) for a in range(ny) for b in range(nz) if (a, b) != (0, 0)), key=far)
+    line = sorted(((a, 0, 0) for a in range(2, nx, 2)), key=far)
+    core = lax.rem(gx, 2)
     partners = []
     for o in DIRS + plane + line:
         o = (o[0] % nx, o[1] % ny, o[2] % nz)
         if o not in partners:
             partners.append(o)
+    partners.sort(key=far)
 
     barrier = pltpu.get_barrier_semaphore()
     for o in partners:
@@ -107,7 +111,7 @@
             packs[k, pl.ds(x, 1), :] = turned[0:1, :]
             packs[k, pl.ds(x + 4, 1), :] = turned[127:128, :]
             return 0
-        lax.fori_loop(0, BX, body, 0)
+        lax.fori_loop(0, BX, body, 0, unroll=True)
 
     loads[0].wait()
     for x in range(BX):
@@ -117,39 +121,35 @@
 
     def state_copies(k):
         copies = []
-        for d in FLAT:
+        for d in DIRS:
+            if d[1]:
+                src = packs.at[k]
+                dst = halos.at[k, 0 if d[1] > 0 else 1, 1 - d[0], 1 - d[2]]
+            else:
+                src = field.at[k, span(d[0], BX, "own"), span(d[2], BZ, "own")]
+                dst = field.at[k, span(-d[0], BX, "halo"), span(-d[2], BZ, "halo")]
             copies.append(pltpu.make_async_remote_copy(
-                src_ref=field.at[k, span(d[0], BX, "own"), span(d[2], BZ, "own")],
-                dst_ref=field.at[k, span(-d[0], BX, "halo"), span(-d[2], BZ, "halo")],
-                send_sem=send_sem.at[k], recv_sem=recv_sem.at[k],
-                device_id=device(d), device_id_type=MESH))
-        for d in TALL:
-            copies.append(pltpu.make_async_remote_copy(
-                src_ref=packs.at[k],
-                dst_ref=halos.at[k, 0 if d[1] > 0 else 1, 1 - d[0], 1 - d[2]],
-                send_sem=send_sem.at[k], recv_sem=recv_sem.at[k],
+                src_ref=src, dst_ref=dst, send_sem=send_sem.at[k], recv_sem=recv_sem.at[k],
                 device_id=device(d), device_id_type=MESH))
         return copies
 
     def out_copies(k):
         copies = []
-        for d in FLAT:
-            if d[0] and d[2]:
-                dst = rc.at[k, pl.ds(0 if d[0] > 0 else 1, 1), pl.ds(0 if d[2] > 0 else 1, 1)]
-            elif d[0]:
-                dst = rx.at[k, pl.ds(0 if d[0] > 0 else 1, 1)]
+        for d in DIRS:
+            at_x, at_z = pl.ds(0 if d[0] > 0 else 1, 1), pl.ds(0 if d[2] > 0 else 1, 1)
+            if d[1]:
+                src = opacks.at[k, 0 if d[1] < 0 else 1]
+                dst = rpacks.at[k, 0 if d[1] > 0 else 1, 1 - d[0], 1 - d[2]]
             else:
-                dst = rz.at[k, :, pl.ds(0 if d[2] > 0 else 1, 1)]
+                src = outs.at[k, span(d[0], BX, "halo"), span(d[2], BZ, "halo")]
+                if d[0] and d[2]:
+                    dst = rc.at[k, at_x, at_z]
+                elif d[0]:
+                    dst = rx.at[k, at_x]
+                else:
+                    dst = rz.at[k, :, at_z]
             copies.append(pltpu.make_async_remote_copy(
-                src_ref=outs.at[k, span(d[0], BX, "halo"), span(d[2], BZ, "halo")],
-                dst_ref=dst,
-                send_sem=send_sem.at[2 + k], recv_sem=recv_sem.at[2 + k],
-                device_id=device(d), device_id_type=MESH))
-        for d in TALL:
-            copies.append(pltpu.make_async_remote_copy(
-                src_ref=opacks.at[k, 0 if d[1] < 0 else 1],
-                dst_ref=rpacks.at[k, 0 if d[1] > 0 else 1, 1 - d[0], 1 - d[2]],
-                send_sem=send_sem.at[2 + k], recv_sem=recv_sem.at[2 + k],
+                src_ref=src, dst_ref=dst, send_sem=send_sem.at[2 + k], recv_sem=recv_sem.at[2 + k],
                 device_id=device(d), device_id_type=MESH))
         return copies
 
@@ -321,7 +321,7 @@
                 for z in range(BZ):
                     field[1, x + 1, z + 1] = field[0, x + 1, z + 1] + mask[z : z + 1] * update[:, z * BY : (z + 1) * BY]
             return 0
-        lax.fori_loop(0, BX, body, 0)
+        lax.fori_loop(0, BX, body, 0, unroll=True)
 
     def cells(k):
         def body(x, _):
@@ -339,7 +339,7 @@
             grads[x, 64:128] = hi
             grads[x, 128:192] = lo
             return 0
-        lax.fori_loop(0, BX, body, 0)
+        lax.fori_loop(0, BX, body, 0, unroll=True)
 
     def adjoint(k):
         def body(x, _):
@@ -350,7 +350,7 @@
                     [zero] + [dp[f * 16 : f * 16 + 16, z * BY : (z + 1) * BY].reshape(1, CH, BY) for z in range(BZ)] + [zero], axis=0)
                 zf[x + 2, f] = q[2:12] - q[0:10] if f == 2 else q[0:10] + 2.0 * q[1:11] + q[2:12]
             return 0
-        lax.fori_loop(0, BX, body, 0)
+        lax.fori_loop(0, BX, body, 0, unroll=True)
 
         def plane_body(xo, _):
             pr = zf[xo + 2, 0] - zf[xo, 0] + zf[xo, 2] + 2.0 * zf[xo + 1, 2] + zf[xo + 2, 2]
@@ -365,7 +365,7 @@
                 opacks[k, s, 0, pl.ds(xo, 1)] = main[r : r + 1]
                 opacks[k, s, 1, pl.ds(xo, 1)] = side[r : r + 1]
             return 0
-        lax.fori_loop(0, BX + 2, plane_body, 0)
+        lax.fori_loop(0, BX + 2, plane_body, 0, unroll=True)
 
     def add_halo(k):
         total = jnp.zeros((8, 128), F32)
@@ -392,7 +392,7 @@
         def body(x, _):
             carried[x] = carried[x] + outs[k, x + 1, pl.ds(1, BZ)] + placed[x * 3].reshape(BZ, CH, BY)
             return 0
-        lax.fori_loop(0, BX, body, 0)
+        lax.fori_loop(0, BX, body, 0, unroll=True)
         for ix in range(2):
             x = 0 if ix == 0 else BX - 1
             m = low_x if ix == 0 else top_x
@@ -411,7 +411,7 @@
             g1 = g1 + dot_nt(percs[k, x, 0:112], grads[x, 64:224])
             g2 = g2 + dot_nt(grads[x, 192:224], hids[k, x, 0:128])
             return g1, g2
-        return lax.fori_loop(0, BX, body, (jnp.zeros((112, 160), F32), jnp.zeros((32, 128), F32)))
+        return lax.fori_loop(0, BX, body, (jnp.zeros((112, 160), F32), jnp.zeros((32, 128), F32)), unroll=True)
 
     wait_rows(FORTH, recv_sem.at[0])
     clear_outside(0)
@@ -451,38 +451,39 @@
     sums[24:32] = jnp.where(left[0:8], both[24:32], bias2)
     sums[32:48] = both[32:48]
 
-    pieces = ny * nz
-    rows = 48 // pieces
-    for p in range(pieces):
-        src1[p, 0:rows] = sums[p * rows : (p + 1) * rows]
+    half = sums.shape[0] // 2
+    own_rows = pl.ds(pl.multiple_of(core * half, 8), half)
+    other_rows = pl.ds(pl.multiple_of((1 - core) * half, 8), half)
+    twin = (gx + 1 - 2 * core, gy, gz)
     mine = gy * nz + gz
-
-    def member(o):
-        _, y, z = device(o)
-        return y * nz + z
-
+    chip = lax.div(gx, 2)
+    pair = pltpu.make_async_remote_copy(
+        src_ref=sums.at[other_rows], dst_ref=rx0, send_sem=ar_send.at[0], recv_sem=ar_recv.at[0],
+        device_id=twin, device_id_type=MESH)
+    pair.start()
+    pair.wait_recv()
+    rx1[mine] = sums[own_rows] + rx0[...]
     stage1 = [pltpu.make_async_remote_copy(
-        src_ref=src1.at[member(o)], dst_ref=rx1.at[i],
-        send_sem=ar_send.at[0], recv_sem=ar_recv.at[0],
-        device_id=device(o), device_id_type=MESH) for i, o in enumerate(plane)]
+        src_ref=rx1.at[mine], dst_ref=rx1.at[mine], send_sem=ar_send.at[1], recv_sem=ar_recv.at[1],
+        device_id=device(o), device_id_type=MESH) for o in plane]
     for c in stage1:
         c.start()
+    pair.wait_send()
     adjoint(0)
     for c in out_copies(0):
         c.start()
-    wait_rows(8 * len(plane), ar_recv.at[0])
-    total = src1[mine]
-    for i in range(len(plane)):
+    wait_rows(half * len(plane), ar_recv.at[1])
+    wait_rows(half * len(plane), ar_send.at[1])
+    total = rx1[0]
+    for i in range(1, ny * nz):
         total = total + rx1[i]
-    rx2[gx] = total
+    rx2[chip] = total
     stage2 = [pltpu.make_async_remote_copy(
-        src_ref=rx2.at[gx], dst_ref=rx2.at[gx],
-        send_sem=ar_send.at[1], recv_sem=ar_recv.at[1],
+        src_ref=rx2.at[chip], dst_ref=rx2.at[chip], send_sem=ar_send.at[2], recv_sem=ar_recv.at[2],
         device_id=device(o), device_id_type=MESH) for o in line]
     for c in stage2:
         c.start()
     wait_rows(BACK, send_sem.at[3])
-    wait_rows(8 * len(plane), ar_send.at[0])
     wait_rows(BACK, recv_sem.at[2])
     add_halo(0)
     for x in range(BX):
@@ -491,25 +492,20 @@
     stores = [pltpu.make_async_copy(a, b, store_sem.at[i]) for i, (a, b) in enumerate((
         (grad_ref, grad_out), (gw1_ref, gw1_out), (gb1_ref, gb1_out), (gw2_ref, gw2_out), (gb2_ref, gb2_out)))]
     stores[0].start()
-    wait_rows(8 * len(line), ar_recv.at[1])
-    wait_rows(8 * len(line), ar_send.at[1])
+    wait_rows(BACK, send_sem.at[2])
+    wait_rows(half * len(line), ar_recv.at[2])
+    wait_rows(half * len(line), ar_send.at[2])
     total = rx2[0]
-    for i in range(1, nx):
+    for i in range(1, nx // 2):
         total = total + rx2[i]
-    rx3[mine] = total
-    stage3 = [pltpu.make_async_remote_copy(
-        src_ref=rx3.at[mine], dst_ref=rx3.at[mine],
-        send_sem=ar_send.at[2], recv_sem=ar_recv.at[2],
-        device_id=device(o), device_id_type=MESH) for o in plane]
-    for c in stage3:
-        c.start()
-    wait_rows(BACK, send_sem.at[2])
-    wait_rows(8 * len(plane), ar_send.at[2])
-    wait_rows(8 * len(plane), ar_recv.at[2])
-    for p in range(pieces):
-        sums[p * rows : (p + 1) * rows] = rx3[p, 0:rows]
+    whole[own_rows] = total
+    share = pltpu.make_async_remote_copy(
+        src_ref=whole.at[own_rows], dst_ref=whole.at[own_rows], send_sem=ar_send.at[3], recv_sem=ar_recv.at[3],
+        device_id=twin, device_id_type=MESH)
+    share.start()
+    share.wait()
     scale = 1.0 / math.sqrt(nx * BX * ny * BY * nz * BZ)
-    final = sums[...] * scale
+    final = whole[...] * scale
     gw1_ref[...] = final[:, 0:64]
     gb1_ref[...] = final[16:17, 64:128]
     gw2_ref[...] = final[0:16, 64:128]
@@ -531,7 +527,6 @@
 
 def body(start_state, cotangent, update_masks, first_weight, first_bias, second_weight, second_bias):
     sizes = (lax.axis_size("gx"), lax.axis_size("gy"), lax.axis_size("gz"))
-    pieces = sizes[1] * sizes[2]
     hbm = pl.BlockSpec(memory_space=pltpu.HBM)
     shapes = ((CH * BX * BZ, BY), (PERC, HID), (1, HID), (CH, HID), (1, CH))
     shapes = tuple(jax.ShapeDtypeStruct(s, F32) for s in shapes)
@@ -572,17 +567,17 @@
         pltpu.VMEM((PERC, 3 * HID), BF16),
         pltpu.VMEM((128, 128), F32),
         pltpu.VMEM((48, 128), F32),
-        pltpu.VMEM((pieces, 8, 128), F32),
-        pltpu.VMEM((pieces, 8, 128), F32),
-        pltpu.VMEM((sizes[0], 8, 128), F32),
-        pltpu.VMEM((pieces, 8, 128), F32),
+        pltpu.VMEM((24, 128), F32),
+        pltpu.VMEM((sizes[1] * sizes[2], 24, 128), F32),
+        pltpu.VMEM((sizes[0] // 2, 24, 128), F32),
+        pltpu.VMEM((48, 128), F32),
         pltpu.VMEM((BACK, 128), F32),
         pltpu.SemaphoreType.DMA((7,)),
         pltpu.SemaphoreType.DMA((5,)),
         pltpu.SemaphoreType.DMA((4,)),
         pltpu.SemaphoreType.DMA((4,)),
-        pltpu.SemaphoreType.DMA((3,)),
-        pltpu.SemaphoreType.DMA((3,)),
+        pltpu.SemaphoreType.DMA((4,)),
+        pltpu.SemaphoreType.DMA((4,)),
     ]
     outs = pl.pallas_call(
         functools.partial(kernel, sizes),

time: 56.2 us -> 45.7 us (0.81)
  Pallas kernels: 55.4 us -> 44.9 us
    pallas_call x1, Pallas kernels: 53.7 us -> 43.2 us  [body(): pl.pallas_call(functools.partial(kernel, sizes), out_shape=shapes, in_spe...]
where the time goes in v3:
time: 45.7 us; the launch traced here: 45.6 us
  Pallas kernels  44.9 us (98%)
  between operations  0.64 us (1%)
    pallas_call x1, Pallas kernels, body(): pl.pallas_call(functools.partial(kernel, sizes), out_shape=shapes, in_spe...  43.2 us
    pallas_call x1, Pallas kernels, body(): pl.pallas_call(write_out, out_shape=shapes, in_specs=[pl.BlockSpec(memory...  1.74 us

profile of v3, /device:TPU:1, one launch (start us, length us, event | category | flops | bytes accessed | tf_op | source)
XLA Modules:
  0.0 45.6 jit_solution(17186393766861181832)
XLA Ops:
  0.6 43.2 %automaton.1 = (f32[512,128]{1,0:T(8,128)}, f32[48,64]{1,0:T(8,128)}, f32[1,64]{1,0:T(1,128)}, f32[16,64]{1,0:T(8,128)}, f32[1,16]{1,0:T(1,128)}) custom-call(f32[512,128]{1,0:T(8,128)} %bitcast.10, f32[512,128]{1,0:T(8,128)} %bitcast.11, s32[64,128]{1,0:T(8,128)} %bitcast.13, f32[48,64]{1,0:T(8,128)} %w1_in.1, f32[1,64]{1,0:T(1,128)} %bitcast.16, ...), custom_call_target="tpu_custom_call" | custom-call | flops 200000000 | bytes 1000000 | tf_op jit(solution)/shard_map/automaton/pallas_call | solution.py:582
  43.8 1.7 %write_out.1 = (f32[512,128]{1,0:T(8,128)}, f32[48,64]{1,0:T(8,128)}, f32[1,64]{1,0:T(1,128)}, f32[16,64]{1,0:T(8,128)}, f32[1,16]{1,0:T(1,128)}) custom-call(f32[512,128]{1,0:T(8,128)} %get-tuple-element.15.refs_0_, f32[48,64]{1,0:T(8,128)} %get-tuple-element.16.refs_1_, f32[1,64]{1,0:T(1,128)} %get-tuple-element.17.refs_2_, ...), custom_call_target="tpu_custom_call" | custom-call | bytes 600000 | tf_op jit(solution)/shard_map/write_out/pallas_call | solution.py:598

commit v4 on v3

--- a/solution.py
+++ b/solution.py
@@ -21,9 +21,11 @@
 
 DIRS = [(dx, dy, dz) for dx in (-1, 0, 1) for dy in (-1, 0, 1) for dz in (-1, 0, 1) if (dx, dy, dz) != (0, 0, 0)]
 DIRS = sorted(DIRS, key=lambda d: -sum(map(abs, d)))
-
-FORTH = 2 * BZ * CH + 2 * BX * CH + 4 * CH + 18 * 8
-BACK = 2 * BZ * CH + 2 * BX * CH + 4 * CH + 18 * 16
+ACROSS = [d for d in DIRS if d[0] != 0]
+WITHIN = [d for d in DIRS if d[0] == 0]
+SIDE_PLANES, MID_PLANES = (0, BX - 1), tuple(range(1, BX - 1))
+
+HALO = 2 * BZ * CH + 2 * BX * CH + 4 * CH + 18 * 8
 
 
 def high(value):
@@ -101,29 +103,35 @@
     not_first = (lane3 > 0).astype(F32)
     not_last = (lane3 < 127).astype(F32)
 
+    def start(copies):
+        for c in copies:
+            c.start()
+
     def wait_rows(rows, sem):
         pltpu.make_async_copy(tally.at[pl.ds(0, rows)], tally.at[pl.ds(0, rows)], sem).wait()
 
-    def pack_state(k):
-        def body(x, _):
-            tile = field[k, x + 1, pl.ds(1, BZ)].reshape(128, 128)
-            turned = tile.T
-            packs[k, pl.ds(x, 1), :] = turned[0:1, :]
-            packs[k, pl.ds(x + 4, 1), :] = turned[127:128, :]
-            return 0
-        lax.fori_loop(0, BX, body, 0, unroll=True)
+    def pack_state(k, x):
+        turned = field[k, x + 1, pl.ds(1, BZ)].reshape(128, 128).T
+        for r, row in ((x, 0), (x + 4, 127)):
+            packs[k, 1, r : r + 1] = turned[row : row + 1]
+            if x in SIDE_PLANES:
+                packs[k, 0, r : r + 1] = turned[row : row + 1]
 
     loads[0].wait()
     for x in range(BX):
         for z in range(BZ):
             field[0, x + 1, z + 1] = state_ref[pl.ds(x * BZ + z, CH, stride=BX * BZ), :]
-    pack_state(0)
-
-    def state_copies(k):
+    for k in range(2):
+        packs[k, 0] = jnp.zeros((8, 128), F32)
+        opacks[k, 0] = jnp.zeros_like(opacks[k, 0])
+    for x in range(BX):
+        pack_state(0, x)
+
+    def state_copies(k, dirs):
         copies = []
-        for d in DIRS:
+        for d in dirs:
             if d[1]:
-                src = packs.at[k]
+                src = packs.at[k, 0 if d[0] else 1]
                 dst = halos.at[k, 0 if d[1] > 0 else 1, 1 - d[0], 1 - d[2]]
             else:
                 src = field.at[k, span(d[0], BX, "own"), span(d[2], BZ, "own")]
@@ -133,12 +141,12 @@
                 device_id=device(d), device_id_type=MESH))
         return copies
 
-    def out_copies(k):
+    def out_copies(k, dirs):
         copies = []
-        for d in DIRS:
+        for d in dirs:
             at_x, at_z = pl.ds(0 if d[0] > 0 else 1, 1), pl.ds(0 if d[2] > 0 else 1, 1)
             if d[1]:
-                src = opacks.at[k, 0 if d[1] < 0 else 1]
+                src = opacks.at[k, 0 if d[0] else 1, 0 if d[1] < 0 else 1, 1 if d[2] else 0]
                 dst = rpacks.at[k, 0 if d[1] > 0 else 1, 1 - d[0], 1 - d[2]]
             else:
                 src = outs.at[k, span(d[0], BX, "halo"), span(d[2], BZ, "halo")]
@@ -154,9 +162,7 @@
         return copies
 
     pl.semaphore_wait(barrier, len(partners))
-    first = state_copies(0)
-    for c in first:
-        c.start()
+    start(state_copies(0, DIRS))
 
     for c in loads[1:5]:
         c.wait()
@@ -285,87 +291,79 @@
             s_below + 2.0 * xs[1] + s_above,
             s_above - s_below], axis=0), 3)
 
-    def forward(k):
-        def body(x, _):
-            zs, zd = [], []
-            for i in range(3):
-                v = field[k, x + i]
-                zs.append(v[0:8] + 2.0 * v[1:9] + v[2:10])
-                zd.append(v[2:10] - v[0:8])
-            b = zs[2] - zs[0]
-            a = zs[0] + 2.0 * zs[1] + zs[2]
-            c = zd[0] + 2.0 * zd[1] + zd[2]
-            up = lambda t: pltpu.roll(t, 127, 2) * not_last
-            down = lambda t: pltpu.roll(t, 1, 2) * not_first
-            features = (
-                2.0 * b + up(b) + down(b),
-                up(a) - down(a),
-                2.0 * c + up(c) + down(c),
-            )
-            for f in range(3):
-                perc = features[f] + placed[x * 3 + f].reshape(BZ, CH, BY)
-                flat = jnp.concatenate([perc[z] for z in range(BZ)], axis=1)
-                hi, lo = halves(flat)
-                percs[k, x, f * 16 : f * 16 + 16] = hi
-                percs[k, x, 48 + f * 16 : 64 + f * 16] = lo
-                percs[k, x, 112 + f * 16 : 128 + f * 16] = hi
-            hid = jnp.tanh(dot(l1[...], percs[k, x]))
-            hidden[k, x] = hid
-            hi, lo = halves(hid)
-            hids[k, x, 0:64] = hi
-            hids[k, x, 64:128] = lo
-            hids[k, x, 144:208] = hi
-            if k == 0:
-                update = dot(l2[...], hids[k, x])
-                mask = mask_ref[pl.ds(pl.multiple_of(x * BZ, 8), BZ), :].astype(F32)
-                for z in range(BZ):
-                    field[1, x + 1, z + 1] = field[0, x + 1, z + 1] + mask[z : z + 1] * update[:, z * BY : (z + 1) * BY]
-            return 0
-        lax.fori_loop(0, BX, body, 0, unroll=True)
-
-    def cells(k):
-        def body(x, _):
-            mask = mask_ref[pl.ds(pl.multiple_of((k * BX + x) * BZ, 8), BZ), :].astype(F32)
-            g = carried[x]
-            du = jnp.concatenate([mask[z : z + 1] * g[z] for z in range(BZ)], axis=1)
-            hi, lo = halves(du)
-            grads[x, 192:208] = hi
-            grads[x, 208:224] = lo
-            grads[x, 224:240] = hi
-            hid = hidden[k, x]
-            dz = dot(l3[...], grads[x, 192:240]) * (1.0 - hid * hid)
-            hi, lo = halves(dz)
-            grads[x, 0:64] = hi
-            grads[x, 64:128] = hi
-            grads[x, 128:192] = lo
-            return 0
-        lax.fori_loop(0, BX, body, 0, unroll=True)
-
-    def adjoint(k):
-        def body(x, _):
-            dp = dot(l4[...], grads[x, 0:192])
-            zero = jnp.zeros((2, CH, BY), F32)
-            for f in range(3):
-                q = jnp.concatenate(
-                    [zero] + [dp[f * 16 : f * 16 + 16, z * BY : (z + 1) * BY].reshape(1, CH, BY) for z in range(BZ)] + [zero], axis=0)
-                zf[x + 2, f] = q[2:12] - q[0:10] if f == 2 else q[0:10] + 2.0 * q[1:11] + q[2:12]
-            return 0
-        lax.fori_loop(0, BX, body, 0, unroll=True)
-
-        def plane_body(xo, _):
-            pr = zf[xo + 2, 0] - zf[xo, 0] + zf[xo, 2] + 2.0 * zf[xo + 1, 2] + zf[xo + 2, 2]
-            q = zf[xo, 1] + 2.0 * zf[xo + 1, 1] + zf[xo + 2, 1]
-            up, down = pr + q, pr - q
-            outs[k, xo] = 2.0 * pr + pltpu.roll(down, 1, 2) * not_first + pltpu.roll(up, 127, 2) * not_last
-            both = jnp.where(lane3 == 0, up, down)
-            main = both[1:9].reshape(128, 128).T
-            side = jnp.concatenate([both[0], both[9]], axis=0)
-            side = jnp.concatenate([side, jnp.zeros((96, 128), F32)], axis=0).T
-            for s, r in ((0, 0), (1, 127)):
-                opacks[k, s, 0, pl.ds(xo, 1)] = main[r : r + 1]
-                opacks[k, s, 1, pl.ds(xo, 1)] = side[r : r + 1]
-            return 0
-        lax.fori_loop(0, BX + 2, plane_body, 0, unroll=True)
+    def forward(k, x):
+        zs, zd = [], []
+        for i in range(3):
+            v = field[k, x + i]
+            zs.append(v[0:8] + 2.0 * v[1:9] + v[2:10])
+            zd.append(v[2:10] - v[0:8])
+        b = zs[2] - zs[0]
+        a = zs[0] + 2.0 * zs[1] + zs[2]
+        c = zd[0] + 2.0 * zd[1] + zd[2]
+        up = lambda t: pltpu.roll(t, 127, 2) * not_last
+        down = lambda t: pltpu.roll(t, 1, 2) * not_first
+        features = (
+            2.0 * b + up(b) + down(b),
+            up(a) - down(a),
+            2.0 * c + up(c) + down(c),
+        )
+        for f in range(3):
+            perc = features[f] + placed[x * 3 + f].reshape(BZ, CH, BY)
+            flat = jnp.concatenate([perc[z] for z in range(BZ)], axis=1)
+            hi, lo = halves(flat)
+            percs[k, x, f * 16 : f * 16 + 16] = hi
+            percs[k, x, 48 + f * 16 : 64 + f * 16] = lo
+            percs[k, x, 112 + f * 16 : 128 + f * 16] = hi
+        hid = jnp.tanh(dot(l1[...], percs[k, x]))
+        hidden[k, x] = hid
+        hi, lo = halves(hid)
+        hids[k, x, 0:64] = hi
+        hids[k, x, 64:128] = lo
+        hids[k, x, 144:208] = hi
+
+    def advance(x):
+        update = dot(l2[...], hids[0, x])
+        mask = mask_ref[x * BZ : (x + 1) * BZ, :].astype(F32)
+        for z in range(BZ):
+            field[1, x + 1, z + 1] = field[0, x + 1, z + 1] + mask[z : z + 1] * update[:, z * BY : (z + 1) * BY]
+        pack_state(1, x)
+
+    def cells(k, x):
+        mask = mask_ref[(k * BX + x) * BZ : (k * BX + x + 1) * BZ, :].astype(F32)
+        g = carried[x]
+        du = jnp.concatenate([mask[z : z + 1] * g[z] for z in range(BZ)], axis=1)
+        hi, lo = halves(du)
+        grads[x, 192:208] = hi
+        grads[x, 208:224] = lo
+        grads[x, 224:240] = hi
+        hid = hidden[k, x]
+        dz = dot(l3[...], grads[x, 192:240]) * (1.0 - hid * hid)
+        hi, lo = halves(dz)
+        grads[x, 0:64] = hi
+        grads[x, 64:128] = hi
+        grads[x, 128:192] = lo
+
+    def spread(x):
+        dp = dot(l4[...], grads[x, 0:192])
+        zero = jnp.zeros((2, CH, BY), F32)
+        for f in range(3):
+            q = jnp.concatenate(
+                [zero] + [dp[f * 16 : f * 16 + 16, z * BY : (z + 1) * BY].reshape(1, CH, BY) for z in range(BZ)] + [zero], axis=0)
+            zf[x + 2, f] = q[2:12] - q[0:10] if f == 2 else q[0:10] + 2.0 * q[1:11] + q[2:12]
+
+    def gather(k, xo):
+        pr = zf[xo + 2, 0] - zf[xo, 0] + zf[xo, 2] + 2.0 * zf[xo + 1, 2] + zf[xo + 2, 2]
+        q = zf[xo, 1] + 2.0 * zf[xo + 1, 1] + zf[xo + 2, 1]
+        up, down = pr + q, pr - q
+        outs[k, xo] = 2.0 * pr + pltpu.roll(down, 1, 2) * not_first + pltpu.roll(up, 127, 2) * not_last
+        both = jnp.where(lane3 == 0, up, down)
+        main = both[1:9].reshape(128, 128).T
+        side = jnp.concatenate([both[0], both[9]], axis=0)
+        side = jnp.concatenate([side, jnp.zeros((96, 128), F32)], axis=0).T
+        tile = 0 if xo in (0, BX + 1) else 1
+        for s, r in ((0, 0), (1, 127)):
+            opacks[k, tile, s, 0, xo : xo + 1] = main[r : r + 1]
+            opacks[k, tile, s, 1, xo : xo + 1] = side[r : r + 1]
 
     def add_halo(k):
         total = jnp.zeros((8, 128), F32)
@@ -376,9 +374,9 @@
                 part = jnp.zeros((8, 128), F32)
                 for iz in range(3):
                     if iz == 1:
-                        t = rpacks[k, iy, ix, iz, 0]
+                        t = rpacks[k, iy, ix, iz]
                     else:
-                        t = pltpu.roll(rpacks[k, iy, ix, iz, 1], 112, 1)
+                        t = pltpu.roll(rpacks[k, iy, ix, iz], 112, 1)
                         t = jnp.where(lane < 16 if iz == 0 else lane >= 112, t, 0.0)
                     part = part + t * (in_y * in_x[ix] * in_z[iz])
                 if ix == 1:
@@ -413,27 +411,42 @@
             return g1, g2
         return lax.fori_loop(0, BX, body, (jnp.zeros((112, 160), F32), jnp.zeros((32, 128), F32)), unroll=True)
 
-    wait_rows(FORTH, recv_sem.at[0])
+    wait_rows(HALO, recv_sem.at[0])
     clear_outside(0)
     filter_columns(0)
-    forward(0)
-    pack_state(1)
-    for c in state_copies(1):
-        c.start()
-    wait_rows(FORTH, send_sem.at[0])
-    wait_rows(FORTH, recv_sem.at[1])
+    for x in SIDE_PLANES:
+        forward(0, x)
+        advance(x)
+    start(state_copies(1, ACROSS))
+    for x in MID_PLANES:
+        forward(0, x)
+        advance(x)
+    start(state_copies(1, WITHIN))
+    wait_rows(HALO, send_sem.at[0])
+    wait_rows(HALO, recv_sem.at[1])
     clear_outside(1)
     filter_columns(1)
-    forward(1)
-    cells(1)
-    adjoint(1)
-    for c in out_copies(1):
-        c.start()
+    for x in SIDE_PLANES:
+        forward(1, x)
+        cells(1, x)
+    for x in SIDE_PLANES:
+        spread(x)
+    gather(1, 0)
+    gather(1, BX + 1)
+    start(out_copies(1, ACROSS))
+    for x in MID_PLANES:
+        forward(1, x)
+        cells(1, x)
+        spread(x)
+    for x in range(BX):
+        gather(1, x + 1)
+    start(out_copies(1, WITHIN))
     ga1, ga2 = weight_grads(1)
-    wait_rows(FORTH, send_sem.at[1])
-    wait_rows(BACK, recv_sem.at[3])
+    wait_rows(HALO, send_sem.at[1])
+    wait_rows(HALO, recv_sem.at[3])
     add_halo(1)
-    cells(0)
+    for x in range(BX):
+        cells(0, x)
     gb1, gb2 = weight_grads(0)
     g1, g2 = ga1 + gb1, ga2 + gb2
 
@@ -466,12 +479,18 @@
     stage1 = [pltpu.make_async_remote_copy(
         src_ref=rx1.at[mine], dst_ref=rx1.at[mine], send_sem=ar_send.at[1], recv_sem=ar_recv.at[1],
         device_id=device(o), device_id_type=MESH) for o in plane]
-    for c in stage1:
-        c.start()
+    start(stage1)
     pair.wait_send()
-    adjoint(0)
-    for c in out_copies(0):
-        c.start()
+    for x in SIDE_PLANES:
+        spread(x)
+    gather(0, 0)
+    gather(0, BX + 1)
+    start(out_copies(0, ACROSS))
+    for x in MID_PLANES:
+        spread(x)
+    for x in range(BX):
+        gather(0, x + 1)
+    start(out_copies(0, WITHIN))
     wait_rows(half * len(plane), ar_recv.at[1])
     wait_rows(half * len(plane), ar_send.at[1])
     total = rx1[0]
@@ -481,10 +500,9 @@
     stage2 = [pltpu.make_async_remote_copy(
         src_ref=rx2.at[chip], dst_ref=rx2.at[chip], send_sem=ar_send.at[2], recv_sem=ar_recv.at[2],
         device_id=device(o), device_id_type=MESH) for o in line]
-    for c in stage2:
-        c.start()
-    wait_rows(BACK, send_sem.at[3])
-    wait_rows(BACK, recv_sem.at[2])
+    start(stage2)
+    wait_rows(HALO, send_sem.at[3])
+    wait_rows(HALO, recv_sem.at[2])
     add_halo(0)
     for x in range(BX):
         for z in range(BZ):
@@ -492,7 +510,7 @@
     stores = [pltpu.make_async_copy(a, b, store_sem.at[i]) for i, (a, b) in enumerate((
         (grad_ref, grad_out), (gw1_ref, gw1_out), (gb1_ref, gb1_out), (gw2_ref, gw2_out), (gb2_ref, gb2_out)))]
     stores[0].start()
-    wait_rows(BACK, send_sem.at[2])
+    wait_rows(HALO, send_sem.at[2])
     wait_rows(half * len(line), ar_recv.at[2])
     wait_rows(half * len(line), ar_send.at[2])
     total = rx2[0]
@@ -544,14 +562,14 @@
         pltpu.VMEM((CH, HID), F32),
         pltpu.VMEM((1, CH), F32),
         pltpu.VMEM((2, BX + 2, BZ + 2, CH, BY), F32),
-        pltpu.VMEM((2, 8, 128), F32),
+        pltpu.VMEM((2, 2, 8, 128), F32),
         pltpu.VMEM((2, 2, 3, 3, 8, 128), F32),
         pltpu.VMEM((2, BX + 2, BZ + 2, CH, BY), F32),
-        pltpu.VMEM((2, 2, 2, 8, 128), F32),
+        pltpu.VMEM((2, 2, 2, 2, 8, 128), F32),
         pltpu.VMEM((2, 2, BZ, CH, BY), F32),
         pltpu.VMEM((2, BX, 2, CH, BY), F32),
         pltpu.VMEM((2, 2, 2, CH, BY), F32),
-        pltpu.VMEM((2, 2, 3, 3, 2, 8, 128), F32),
+        pltpu.VMEM((2, 2, 3, 3, 8, 128), F32),
         pltpu.VMEM((2, BX, P_ROWS, ROW), BF16),
         pltpu.VMEM((2, BX, H_ROWS, ROW), BF16),
         pltpu.VMEM((2, BX, HID, ROW), F32),
@@ -571,7 +589,7 @@
         pltpu.VMEM((sizes[1] * sizes[2], 24, 128), F32),
         pltpu.VMEM((sizes[0] // 2, 24, 128), F32),
         pltpu.VMEM((48, 128), F32),
-        pltpu.VMEM((BACK, 128), F32),
+        pltpu.VMEM((HALO, 128), F32),
         pltpu.SemaphoreType.DMA((7,)),
         pltpu.SemaphoreType.DMA((5,)),
         pltpu.SemaphoreType.DMA((4,)),

time: 45.7 us -> 44.8 us (0.980)
  Pallas kernels: 44.9 us -> 44.1 us
    pallas_call x1, Pallas kernels: 43.2 us -> 42.3 us  [body(): pl.pallas_call(functools.partial(kernel, sizes), out_shape=shapes, in_spe...]
where the time goes in v4:
time: 44.8 us; the launch traced here: 44.7 us
  Pallas kernels  44.1 us (98%)
  between operations  0.64 us (1%)
    pallas_call x1, Pallas kernels, body(): pl.pallas_call(functools.partial(kernel, sizes), out_shape=shapes, in_spe...  42.3 us
    pallas_call x1, Pallas kernels, body(): pl.pallas_call(write_out, out_shape=shapes, in_specs=[pl.BlockSpec(memory...  1.74 us

profile of v4, /device:TPU:1, one launch (start us, length us, event | category | flops | bytes accessed | tf_op | source)
XLA Modules:
  0.0 44.7 jit_solution(15262976847231910951)
XLA Ops:
  0.6 42.3 %automaton.1 = (f32[512,128]{1,0:T(8,128)}, f32[48,64]{1,0:T(8,128)}, f32[1,64]{1,0:T(1,128)}, f32[16,64]{1,0:T(8,128)}, f32[1,16]{1,0:T(1,128)}) custom-call(f32[512,128]{1,0:T(8,128)} %bitcast.10, f32[512,128]{1,0:T(8,128)} %bitcast.11, s32[64,128]{1,0:T(8,128)} %bitcast.13, f32[48,64]{1,0:T(8,128)} %w1_in.1, f32[1,64]{1,0:T(1,128)} %bitcast.16, ...), custom_call_target="tpu_custom_call" | custom-call | flops 200000000 | bytes 1000000 | tf_op jit(solution)/shard_map/automaton/pallas_call | solution.py:600
  43.0 1.7 %write_out.1 = (f32[512,128]{1,0:T(8,128)}, f32[48,64]{1,0:T(8,128)}, f32[1,64]{1,0:T(1,128)}, f32[16,64]{1,0:T(8,128)}, f32[1,16]{1,0:T(1,128)}) custom-call(f32[512,128]{1,0:T(8,128)} %get-tuple-element.15.refs_0_, f32[48,64]{1,0:T(8,128)} %get-tuple-element.16.refs_1_, f32[1,64]{1,0:T(1,128)} %get-tuple-element.17.refs_2_, ...), custom_call_target="tpu_custom_call" | custom-call | bytes 600000 | tf_op jit(solution)/shard_map/write_out/pallas_call | solution.py:616

commit v5 on v4

--- a/solution.py
+++ b/solution.py
@@ -57,12 +57,12 @@
 def kernel(
     sizes,
     state_in, cot_in, mask_in, w1_in, b1_in, w2_in, b2_in,
-    grad_out, gw1_out, gb1_out, gw2_out, gb2_out,
-    grad_ref, gw1_ref, gb1_ref, gw2_ref, gb2_ref,
+    grad_out, sums_out,
+    grad_ref,
     state_ref, cot_ref, mask_ref, w1_ref, b1_ref, w2_ref, b2_ref,
     field, packs, halos, outs, opacks, rx, rz, rc, rpacks,
     percs, hids, hidden, grads, carried, zf, placed, onehot,
-    tall, l1, l2, l3, l4, turn, sums, rx0, rx1, rx2, whole,
+    tall, l1, l2, l3, l4, turn, sums, rx0, rx1, rx2, whole, zline,
     tally, load_sem, store_sem, send_sem, recv_sem, ar_send, ar_recv,
 ):
     nx, ny, nz = sizes
@@ -291,12 +291,20 @@
             s_below + 2.0 * xs[1] + s_above,
             s_above - s_below], axis=0), 3)
 
+    ready = set()
+
     def forward(k, x):
         zs, zd = [], []
-        for i in range(3):
-            v = field[k, x + i]
-            zs.append(v[0:8] + 2.0 * v[1:9] + v[2:10])
-            zd.append(v[2:10] - v[0:8])
+        for i in range(x, x + 3):
+            if (k, i) not in ready:
+                ready.add((k, i))
+                v = field[k, i]
+                zs.append(v[0:8] + 2.0 * v[1:9] + v[2:10])
+                zd.append(v[2:10] - v[0:8])
+                zline[i, 0], zline[i, 1] = zs[-1], zd[-1]
+            else:
+                zs.append(zline[i, 0])
+                zd.append(zline[i, 1])
         b = zs[2] - zs[0]
         a = zs[0] + 2.0 * zs[1] + zs[2]
         c = zd[0] + 2.0 * zd[1] + zd[2]
@@ -508,7 +516,7 @@
         for z in range(BZ):
             grad_ref[pl.ds(x * BZ + z, CH, stride=BX * BZ), :] = carried[x, z]
     stores = [pltpu.make_async_copy(a, b, store_sem.at[i]) for i, (a, b) in enumerate((
-        (grad_ref, grad_out), (gw1_ref, gw1_out), (gb1_ref, gb1_out), (gw2_ref, gw2_out), (gb2_ref, gb2_out)))]
+        (grad_ref, grad_out), (whole, sums_out)))]
     stores[0].start()
     wait_rows(HALO, send_sem.at[2])
     wait_rows(half * len(line), ar_recv.at[2])
@@ -522,22 +530,22 @@
         device_id=twin, device_id_type=MESH)
     share.start()
     share.wait()
-    scale = 1.0 / math.sqrt(nx * BX * ny * BY * nz * BZ)
-    final = whole[...] * scale
-    gw1_ref[...] = final[:, 0:64]
-    gb1_ref[...] = final[16:17, 64:128]
-    gw2_ref[...] = final[0:16, 64:128]
-    gb2_ref[...] = final[24:25, 64:80]
     for c in stores[1:]:
         c.start()
     for c in stores:
         c.wait()
 
 
-def write_out(*refs):
-    sems = refs[-1]
-    copies = [pltpu.make_async_copy(refs[i], refs[5 + i], sems.at[i]) for i in range(5)]
-    for c in copies:
+def write_out(scale, grad, sums, grad_out, gw1_out, gb1_out, gw2_out, gb2_out, gw1, gb1, gw2, gb2, sems):
+    copies = [pltpu.make_async_copy(a, b, sems.at[i]) for i, (a, b) in enumerate((
+        (grad, grad_out), (gw1, gw1_out), (gb1, gb1_out), (gw2, gw2_out), (gb2, gb2_out)))]
+    copies[0].start()
+    final = sums[...] * scale
+    gw1[...] = final[:, 0:64]
+    gb1[...] = final[16:17, 64:128]
+    gw2[...] = final[0:16, 64:128]
+    gb2[...] = final[24:25, 64:80]
+    for c in copies[1:]:
         c.start()
     for c in copies:
         c.wait()
@@ -550,10 +558,6 @@
     shapes = tuple(jax.ShapeDtypeStruct(s, F32) for s in shapes)
     scratch = [
         pltpu.VMEM((CH * BX * BZ, BY), F32),
-        pltpu.VMEM((PERC, HID), F32),
-        pltpu.VMEM((1, HID), F32),
-        pltpu.VMEM((CH, HID), F32),
-        pltpu.VMEM((1, CH), F32),
         pltpu.VMEM((CH * BX * BZ, BY), F32),
         pltpu.VMEM((CH * BX * BZ, BY), F32),
         pltpu.VMEM((2 * BX * BZ, BY), jnp.int32),
@@ -589,9 +593,10 @@
         pltpu.VMEM((sizes[1] * sizes[2], 24, 128), F32),
         pltpu.VMEM((sizes[0] // 2, 24, 128), F32),
         pltpu.VMEM((48, 128), F32),
+        pltpu.VMEM((BX + 2, 2, BZ, CH, BY), F32),
         pltpu.VMEM((HALO, 128), F32),
         pltpu.SemaphoreType.DMA((7,)),
-        pltpu.SemaphoreType.DMA((5,)),
+        pltpu.SemaphoreType.DMA((2,)),
         pltpu.SemaphoreType.DMA((4,)),
         pltpu.SemaphoreType.DMA((4,)),
         pltpu.SemaphoreType.DMA((4,)),
@@ -599,9 +604,9 @@
     ]
     outs = pl.pallas_call(
         functools.partial(kernel, sizes),
-        out_shape=shapes,
+        out_shape=(shapes[0], jax.ShapeDtypeStruct((PERC, 128), F32)),
         in_specs=[hbm] * 7,
-        out_specs=(hbm,) * 5,
+        out_specs=(hbm,) * 2,
         scratch_shapes=scratch,
         compiler_params=pltpu.CompilerParams(
             collective_id=0, has_side_effects=True, vmem_limit_bytes=60 * 1024 * 1024),
@@ -614,11 +619,11 @@
         first_weight, first_bias.reshape(1, HID), second_weight.T, second_bias.reshape(1, CH),
     )
     grad, gw1, gb1, gw2, gb2 = pl.pallas_call(
-        write_out,
+        functools.partial(write_out, 1.0 / math.sqrt(sizes[0] * BX * sizes[1] * BY * sizes[2] * BZ)),
         out_shape=shapes,
-        in_specs=[pl.BlockSpec(memory_space=pltpu.VMEM)] * 5,
+        in_specs=[pl.BlockSpec(memory_space=pltpu.VMEM)] * 2,
         out_specs=(hbm,) * 5,
-        scratch_shapes=[pltpu.SemaphoreType.DMA((5,))],
+        scratch_shapes=[pltpu.VMEM(s.shape, F32) for s in shapes[1:]] + [pltpu.SemaphoreType.DMA((5,))],
         cost_estimate=pl.CostEstimate(flops=0, bytes_accessed=600000, transcendentals=0),
         name="write_out",
     )(*outs)

time: 44.8 us -> 44.7 us (level)
  no operation moved by 1% of the time
where the time goes in v5:
time: 44.7 us; the launch traced here: 44.5 us
  Pallas kernels  43.9 us (98%)
  between operations  0.64 us (1%)
    pallas_call x1, Pallas kernels, body(): pl.pallas_call(functools.partial(kernel, sizes), out_shape=(shapes[0], ja...  42.2 us
    pallas_call x1, Pallas kernels, body(): pl.pallas_call(functools.partial(write_out, 1.0 / math.sqrt(sizes[0] * BX...  1.71 us

profile of v5, /device:TPU:1, one launch (start us, length us, event | category | flops | bytes accessed | tf_op | source)
XLA Modules:
  0.0 44.5 jit_solution(3911210387061993126)
XLA Ops:
  0.6 42.2 %automaton.1 = (f32[512,128]{1,0:T(8,128)}, f32[48,128]{1,0:T(8,128)}) custom-call(f32[512,128]{1,0:T(8,128)} %bitcast.10, f32[512,128]{1,0:T(8,128)} %bitcast.11, s32[64,128]{1,0:T(8,128)} %bitcast.13, f32[48,64]{1,0:T(8,128)} %w1_in.1, f32[1,64]{1,0:T(1,128)} %bitcast.16, f32[16,64]{1,0:T(8,128)} %bitcast.14, f32[1,16]{1,0:T(1,128)} %bitcast.17), custom_call_target="tpu_custom_call" | custom-call | flops 200000000 | bytes 1000000 | tf_op jit(solution)/shard_map/automaton/pallas_call | solution.py:605
  42.8 1.7 %write_out.1 = (f32[512,128]{1,0:T(8,128)}, f32[48,64]{1,0:T(8,128)}, f32[1,64]{1,0:T(1,128)}, f32[16,64]{1,0:T(8,128)}, f32[1,16]{1,0:T(1,128)}) custom-call(f32[512,128]{1,0:T(8,128)} %get-tuple-element.12.grad, f32[48,128]{1,0:T(8,128)} %get-tuple-element.13.sums), custom_call_target="tpu_custom_call" | custom-call | bytes 600000 | tf_op jit(solution)/shard_map/write_out/pallas_call | solution.py:621

commit v6 on v5

--- a/solution.py
+++ b/solution.py
@@ -123,7 +123,7 @@
             field[0, x + 1, z + 1] = state_ref[pl.ds(x * BZ + z, CH, stride=BX * BZ), :]
     for k in range(2):
         packs[k, 0] = jnp.zeros((8, 128), F32)
-        opacks[k, 0] = jnp.zeros_like(opacks[k, 0])
+        opacks[k] = jnp.zeros_like(opacks[k])
     for x in range(BX):
         pack_state(0, x)
 
@@ -367,11 +367,11 @@
         both = jnp.where(lane3 == 0, up, down)
         main = both[1:9].reshape(128, 128).T
         side = jnp.concatenate([both[0], both[9]], axis=0)
-        side = jnp.concatenate([side, jnp.zeros((96, 128), F32)], axis=0).T
+        side = side.T
         tile = 0 if xo in (0, BX + 1) else 1
         for s, r in ((0, 0), (1, 127)):
             opacks[k, tile, s, 0, xo : xo + 1] = main[r : r + 1]
-            opacks[k, tile, s, 1, xo : xo + 1] = side[r : r + 1]
+            opacks[k, tile, s, 1, xo : xo + 1, 0:32] = side[r : r + 1]
 
     def add_halo(k):
         total = jnp.zeros((8, 128), F32)

time: 44.7 us -> 44.7 us (level)
  no operation moved by 1% of the time
where the time goes in v6:
time: 44.7 us; the launch traced here: 44.6 us
  Pallas kernels  43.9 us (98%)
  between operations  0.64 us (1%)
    pallas_call x1, Pallas kernels, body(): pl.pallas_call(functools.partial(kernel, sizes), out_shape=(shapes[0], ja...  42.2 us
    pallas_call x1, Pallas kernels, body(): pl.pallas_call(functools.partial(write_out, 1.0 / math.sqrt(sizes[0] * BX...  1.71 us

profile of v6, /device:TPU:1, one launch (start us, length us, event | category | flops | bytes accessed | tf_op | source)
XLA Modules:
  0.0 44.6 jit_solution(5547489776389448749)
XLA Ops:
  0.6 42.2 %automaton.1 = (f32[512,128]{1,0:T(8,128)}, f32[48,128]{1,0:T(8,128)}) custom-call(f32[512,128]{1,0:T(8,128)} %bitcast.10, f32[512,128]{1,0:T(8,128)} %bitcast.11, s32[64,128]{1,0:T(8,128)} %bitcast.13, f32[48,64]{1,0:T(8,128)} %w1_in.1, f32[1,64]{1,0:T(1,128)} %bitcast.16, f32[16,64]{1,0:T(8,128)} %bitcast.14, f32[1,16]{1,0:T(1,128)} %bitcast.17), custom_call_target="tpu_custom_call" | custom-call | flops 200000000 | bytes 1000000 | tf_op jit(solution)/shard_map/automaton/pallas_call | solution.py:605
  42.8 1.7 %write_out.1 = (f32[512,128]{1,0:T(8,128)}, f32[48,64]{1,0:T(8,128)}, f32[1,64]{1,0:T(1,128)}, f32[16,64]{1,0:T(8,128)}, f32[1,16]{1,0:T(1,128)}) custom-call(f32[512,128]{1,0:T(8,128)} %get-tuple-element.12.grad, f32[48,128]{1,0:T(8,128)} %get-tuple-element.13.sums), custom_call_target="tpu_custom_call" | custom-call | bytes 600000 | tf_op jit(solution)/shard_map/write_out/pallas_call | solution.py:621
